TPU v7x, 256 devices: a whole 4x4x8 slice. The times are simulated.
256 devices in a mesh: ctx: 64 (over z_lo, y, x, core), ch: 4 (over z_hi).
Axes of the slice: x: 4, y: 4, z: 8 (z_hi: 4, z_lo: 2; z = z_hi * 2 + z_lo), core: 2. Of those that a mesh axis runs over, the one named last changes fastest.
Arguments:
- queries: bfloat16 [8192, 16384], P('ch', 'ctx'), may hold values from -6 to 6
- keys: bfloat16 [8192, 16384], P('ch', 'ctx'), may hold values from -6 to 6
- values: bfloat16 [8192, 16384], P('ch', 'ctx'), may hold values from -6 to 6
- short_taps: float32 [3, 7, 8192], P(None, None, 'ch'), may hold values from -2 to 2
- long_filter: bfloat16 [4, 2048, 16384], P('ch', 'ctx'), may hold values from -1.5 to 1.5
- skip_gain: float32 [4, 2048], P('ch', 'ctx'), may hold values from 0.5 to 1.5
Outputs:
- mixed: bfloat16 [8192, 16384], P('ch', 'ctx')
All inputs are finite; a program needn't handle non-finite values.
Results may differ from a plain program's by a relative error of at most 0.01.
Values may be sent and summed in bfloat16 or wider, within the bound.
No kernel may reach another device: no remote copies, remote signals or barrier semaphores. Data moves between devices by JAX's collectives and lax.ppermute only.
A program may use at most 64 MiB of HBM per device.

v0:
```python
import functools

import jax
import jax.numpy as jnp
import numpy as np
from jax import lax
from jax.experimental import pallas as pl
from jax.experimental.pallas import tpu as pltpu
from jax.sharding import PartitionSpec as P

VMEM_LIMIT = 48 * 1024 * 1024
RIM = 8
BF16, F32 = jnp.bfloat16, jnp.float32


def head_and_rest(table):
    head = table.astype(np.float32).astype(jnp.bfloat16)
    rest = (table - head.astype(np.float64)).astype(np.float32).astype(jnp.bfloat16)
    return head, rest


def transform_tables(side, runs):
    length = side * side
    k = np.arange(side)
    natural = np.arange(side)
    blocks = side // runs
    held = (np.arange(blocks)[None, :] * runs + np.arange(runs)[:, None]).reshape(-1)

    def first(order):
        angle = 2 * np.pi * (k[:, None] + 0.25) * order[None, :] / side
        both = np.concatenate([np.cos(angle), np.sin(angle)], axis=0)
        return np.concatenate(head_and_rest(both), axis=1)

    turn = 2 * np.pi * (k[:, None] + 0.25) * natural[None, :] / length
    twist = np.stack([np.cos(turn), np.sin(turn)]).astype(np.float32)
    angle = 2 * np.pi * (natural[:, None] * k[None, :] % side) / side
    cos, sin = np.cos(angle), np.sin(angle)

    def second(matrix):
        head, rest = head_and_rest(matrix)
        return np.concatenate([head, head, rest], axis=0)

    ahead = second(np.block([[cos, sin], [-sin, cos]]))
    back = second(np.block([[cos, -sin], [sin, cos]]))
    angle = 2 * np.pi * held[:, None] * (k[None, :] + 0.25) / side
    head, rest = head_and_rest(np.concatenate([np.cos(angle), np.sin(angle)], axis=1) / length)
    last = np.concatenate([head, head, rest], axis=1)
    return first(natural), first(held), twist, ahead, back, last


def split(array):
    head = array.astype(BF16)
    return head, (array - head.astype(F32)).astype(BF16)


def dot(a, b):
    return jnp.dot(a, b, preferred_element_type=F32)


def tail_kernel(k_ref, v_ref, q_ref, out_ref):
    parts = [ref[...].astype(F32).T[-RIM:] for ref in (k_ref, v_ref, q_ref)]
    parts.append(jnp.zeros_like(parts[0]))
    out_ref[...] = jnp.concatenate(parts, axis=0).astype(BF16)


def short_conv(source, halo, taps_ref, which, ext):
    count = source.shape[1]
    ext[:RIM] = halo
    ext[RIM:] = source.astype(F32).T
    total = taps_ref[which, 0:1] * ext[RIM : RIM + count]
    for j in range(1, taps_ref.shape[1]):
        total = total + taps_ref[which, j : j + 1] * ext[RIM - j : RIM - j + count]
    return total


def gate_kernel(k_ref, v_ref, halo_ref, taps_ref, out_ref, k_ext, v_ext):
    halo = halo_ref[...].astype(F32)
    keys = short_conv(k_ref[...], halo[:RIM], taps_ref, 1, k_ext)
    values = short_conv(v_ref[...], halo[RIM : 2 * RIM], taps_ref, 2, v_ext)
    out_ref[...] = (keys * values).T.astype(BF16)


def query_kernel(q_ref, halo_ref, taps_ref, out_ref, q_ext):
    halo = halo_ref[...].astype(F32)
    queries = short_conv(q_ref[...], halo[2 * RIM : 3 * RIM], taps_ref, 0, q_ext)
    out_ref[...] = queries.T.astype(BF16)


def to_spectrum(pairs, first, twist, ahead):
    side = twist.shape[1]
    cos, sin = twist[0], twist[1]
    stacked = []
    for pair in pairs:
        both = dot(first, jnp.concatenate([pair, pair], axis=0))
        for i in range(2):
            re = both[:side, i * side : (i + 1) * side]
            im = both[side:, i * side : (i + 1) * side]
            turned = jnp.concatenate([re * cos - im * sin, re * sin + im * cos], axis=1)
            head, rest = split(turned)
            stacked.append(jnp.concatenate([head, rest, head], axis=1))
    return dot(jnp.concatenate(stacked, axis=0), ahead)


def filter_kernel(filt_ref, gain_ref, first_ref, twist_ref, ahead_ref, out_ref):
    count, side, _ = filt_ref.shape
    pairs = [
        jnp.concatenate([filt_ref[c], filt_ref[c + 1]], axis=1) for c in range(0, count, 2)
    ]
    spectrum = to_spectrum(pairs, first_ref[...], twist_ref, ahead_ref[...])
    base = pl.program_id(0) * count
    for c in range(count):
        rows = spectrum[c * side : (c + 1) * side]
        re, im = rows[:, :side] + gain_ref[0, base + c], rows[:, side:]
        out_ref[c] = jnp.concatenate([re, im], axis=1)


def long_kernel(
    x_ref, filt_ref, first_ref, twist_ref, ahead_ref, back_ref, last_ref, out_ref, x_wide, y_wide
):
    blocks, owned, width = x_ref.shape
    count, side, _ = filt_ref.shape
    step = pl.program_id(0)

    @pl.when(step == 0)
    def _():
        for i in range(x_wide.shape[0]):
            piece = x_ref[:, :, i * side : (i + 1) * side]
            x_wide[i] = piece.astype(F32).reshape(blocks * owned, side)

    cos, sin = twist_ref[0], twist_ref[1]
    runs = width // side
    held = []
    for c in range(count):
        rows = [
            x_wide[i, pl.ds(step * count + c, blocks, stride=owned), :] for i in range(runs)
        ]
        held.append(jnp.concatenate(rows, axis=0).astype(BF16))
    pairs = [jnp.concatenate(held[c : c + 2], axis=1) for c in range(0, count, 2)]
    spectrum = to_spectrum(pairs, first_ref[...], twist_ref, ahead_ref[...])
    stacked = []
    for c in range(count):
        rows = spectrum[c * side : (c + 1) * side]
        re, im = rows[:, :side], rows[:, side:]
        fre, fim = filt_ref[c, :, :side], filt_ref[c, :, side:]
        head, rest = split(jnp.concatenate([re * fre - im * fim, re * fim + im * fre], axis=1))
        stacked.append(jnp.concatenate([head, rest, head], axis=1))
    undone = dot(jnp.concatenate(stacked, axis=0), back_ref[...])
    for c in range(0, count, 2):
        columns = []
        for i in (c, c + 1):
            rows = undone[i * side : (i + 1) * side]
            re, im = rows[:, :side], rows[:, side:]
            turned = jnp.concatenate([re * cos + im * sin, im * cos - re * sin], axis=0)
            head, rest = split(turned)
            columns.append(jnp.concatenate([head, rest, head], axis=0))
        result = dot(last_ref[...], jnp.concatenate(columns, axis=1))
        for i in range(2):
            for j in range(runs):
                y_wide[j, pl.ds(step * count + c + i, blocks, stride=owned), :] = result[
                    j * blocks : (j + 1) * blocks, i * side : (i + 1) * side
                ]

    @pl.when(step == pl.num_programs(0) - 1)
    def _():
        for j in range(runs):
            out_ref[:, :, j * side : (j + 1) * side] = (
                y_wide[j].astype(BF16).reshape(blocks, owned, side)
            )


def params():
    return pltpu.CompilerParams(vmem_limit_bytes=VMEM_LIMIT)


def local(queries, keys, values, short_taps, long_filter, skip_gain):
    ctx_count = lax.axis_size("ctx")
    width, tokens = queries.shape
    owned = width // ctx_count
    side = 128
    runs = tokens // side
    first_plain, first_held, twist, ahead, back, last = (
        jnp.asarray(t) for t in transform_tables(side, runs)
    )
    n_taps = short_taps.shape[1]

    rows = 512
    tail_spec = pl.BlockSpec((rows, 128), lambda i: (i, tokens // 128 - 1))
    with jax.named_scope("tail"):
        tail = pl.pallas_call(
            tail_kernel,
            grid=(width // rows,),
            in_specs=[tail_spec] * 3,
            out_specs=pl.BlockSpec((4 * RIM, rows), lambda i: (0, i)),
            out_shape=jax.ShapeDtypeStruct((4 * RIM, width), BF16),
            compiler_params=params(),
        )(keys, values, queries)
    halo = lax.ppermute(tail, "ctx", [(i, i + 1) for i in range(ctx_count - 1)])

    rows = 256
    data_spec = pl.BlockSpec((rows, tokens), lambda i: (i, 0))
    halo_spec = pl.BlockSpec((4 * RIM, rows), lambda i: (0, i))
    taps_spec = pl.BlockSpec((3, n_taps, rows), lambda i: (0, 0, i))
    ext = pltpu.VMEM((RIM + tokens, rows), F32)
    with jax.named_scope("gate"):
        gated = pl.pallas_call(
            gate_kernel,
            grid=(width // rows,),
            in_specs=[data_spec, data_spec, halo_spec, taps_spec],
            out_specs=data_spec,
            out_shape=jax.ShapeDtypeStruct((width, tokens), BF16),
            scratch_shapes=[ext, ext],
            compiler_params=params(),
            cost_estimate=pl.CostEstimate(
                flops=30 * width * tokens, bytes_accessed=6 * width * tokens, transcendentals=0
            ),
        )(keys, values, halo, short_taps)
    arrived = lax.all_to_all(
        gated.reshape(ctx_count, owned, tokens), "ctx", split_axis=0, concat_axis=0, tiled=True
    )
    with jax.named_scope("query"):
        q_short = pl.pallas_call(
            query_kernel,
            grid=(width // rows,),
            in_specs=[data_spec, halo_spec, taps_spec],
            out_specs=data_spec,
            out_shape=jax.ShapeDtypeStruct((width, tokens), BF16),
            scratch_shapes=[ext],
            compiler_params=params(),
            cost_estimate=pl.CostEstimate(
                flops=15 * width * tokens, bytes_accessed=4 * width * tokens, transcendentals=0
            ),
        )(queries, halo, short_taps)

    count = 4
    whole = pl.BlockSpec(memory_space=pltpu.VMEM)
    spectrum_spec = pl.BlockSpec((count, side, 2 * side), lambda i: (i, 0, 0))
    with jax.named_scope("filter"):
        spectrum = pl.pallas_call(
            filter_kernel,
            grid=(owned // count,),
            in_specs=[
                pl.BlockSpec((count, side, side), lambda i: (i, 0, 0)),
                pl.BlockSpec(memory_space=pltpu.SMEM),
                whole,
                whole,
                whole,
            ],
            out_specs=spectrum_spec,
            out_shape=jax.ShapeDtypeStruct((owned, side, 2 * side), F32),
            compiler_params=params(),
            cost_estimate=pl.CostEstimate(
                flops=owned * side * side * side * 16, bytes_accessed=5 << 20, transcendentals=0
            ),
        )(long_filter.reshape(owned, side, side), skip_gain, first_plain, twist, ahead)
    wide = pltpu.VMEM((runs, ctx_count * owned, side), F32)
    with jax.named_scope("long"):
        long = pl.pallas_call(
            long_kernel,
            grid=(owned // count,),
            in_specs=[whole, spectrum_spec, whole, whole, whole, whole, whole],
            out_specs=pl.BlockSpec((ctx_count, owned, tokens), lambda i: (0, 0, 0)),
            out_shape=jax.ShapeDtypeStruct((ctx_count, owned, tokens), BF16),
            scratch_shapes=[wide, wide],
            compiler_params=params(),
            cost_estimate=pl.CostEstimate(
                flops=owned * side * side * side * 32, bytes_accessed=7 << 20, transcendentals=0
            ),
        )(arrived, spectrum, first_held, twist, ahead, back, last)
    returned = lax.all_to_all(long, "ctx", split_axis=0, concat_axis=0, tiled=True)
    returned = returned.reshape(width, tokens)
    return (q_short.astype(F32) * returned.astype(F32)).astype(BF16)


def solution(mesh):
    placed = (
        P("ch", "ctx"),
        P("ch", "ctx"),
        P("ch", "ctx"),
        P(None, None, "ch"),
        P("ch", "ctx", None),
        P("ch", "ctx"),
    )
    return jax.shard_map(
        local, mesh=mesh, in_specs=placed, out_specs=P("ch", "ctx"), check_vma=False
    )
```

profile of v0, /device:TPU:1, one launch (start us, length us, event | category | flops | bytes accessed | tf_op | source)
XLA Modules:
  0.0 83.5 jit_solution(10407815813337924875)
XLA Ops:
  0.0 1.2 %copy-done = bf16[2048,256]{1,0:T(8,128)(2,1)S(1)} copy-done((bf16[2048,256]{1,0:T(8,128)(2,1)S(1)}, bf16[2048,256]{1,0:T(8,128)(2,1)}, u32[]{:S(2)}) %copy-start) | copy-done | bytes 1048600
  1.2 1.2 %copy-done.2 = bf16[2048,256]{1,0:T(8,128)(2,1)S(1)} copy-done((bf16[2048,256]{1,0:T(8,128)(2,1)S(1)}, bf16[2048,256]{1,0:T(8,128)(2,1)}, u32[]{:S(2)}) %copy-start.2) | copy-done | bytes 1048600
  2.5 1.2 %copy-done.3 = bf16[2048,256]{1,0:T(8,128)(2,1)S(1)} copy-done((bf16[2048,256]{1,0:T(8,128)(2,1)S(1)}, bf16[2048,256]{1,0:T(8,128)(2,1)}, u32[]{:S(2)}) %copy-start.3) | copy-done | bytes 1048600
  3.7 1.0 %tail.1 = bf16[32,2048]{1,0:T(8,128)(2,1)S(1)} custom-call(bf16[2048,256]{1,0:T(8,128)(2,1)S(1)} %copy-done.2, bf16[2048,256]{1,0:T(8,128)(2,1)S(1)} %copy-done.3, bf16[2048,256]{1,0:T(8,128)(2,1)S(1)} %copy-done), custom_call_target="tpu_custom_call" | custom-call | tf_op jit(solution)/shard_map/tail/pallas_call | solution.py:189
  4.7 0.0 copy-start.13
  4.7 4.6 %collective-permute-start = (bf16[32,2048]{1,0:T(8,128)(2,1)S(1)}, bf16[32,2048]{1,0:T(8,128)(2,1)S(1)}, u32[]{:S(2)}, u32[]{:S(2)}) collective-permute-start(bf16[32,2048]{1,0:T(8,128)(2,1)S(1)} %tail.1), channel_id=1, source_target_pairs={{0,4},{4,8},{8,12},{12,16},{16,20},{20,24},{24,28},{28,32},{32,36}... | collective-permute-start | bytes 393224 | tf_op jit(solution)/shard_map/ppermute | solution.py:197
  9.4 1.9 %collective-permute-done.halo_ref = bf16[32,2048]{1,0:T(8,128)(2,1)S(1)} collective-permute-done((bf16[32,2048]{1,0:T(8,128)(2,1)S(1)}, bf16[32,2048]{1,0:T(8,128)(2,1)S(1)}, u32[]{:S(2)}, u32[]{:S(2)}) %collective-permute-start) | collective-permute-done | bytes 131104 | tf_op jit(solution)/shard_map/ppermute | solution.py:197
  11.3 0.0 copy-done.5
  11.3 6.5 %gate.1 = bf16[2048,256]{1,0:T(8,128)(2,1)} custom-call(bf16[2048,256]{1,0:T(8,128)(2,1)S(1)} %copy-done.2, bf16[2048,256]{1,0:T(8,128)(2,1)S(1)} %copy-done.3, bf16[32,2048]{1,0:T(8,128)(2,1)S(1)} %collective-permute-done.halo_ref, f32[3,7,2048]{2,1,0:T(8,128)S(1)} %copy-done.5), custom_call_target="tpu_custom_call" | custom-call | flops 15728640 | bytes 3145728 | tf_op jit(solution)/shard_map/gate/pallas_call | solution.py:205
  17.8 10.3 %all-to-all-start = ((bf16[64,32,256]{2,1,0:T(8,128)(2,1)}), bf16[64,32,256]{2,1,0:T(8,128)(2,1)S(1)}, u32[]{:S(2)}, u32[]{:S(2)}) async-start(bf16[64,32,256]{2,1,0:T(8,128)(2,1)} %bitcast), calls=%async_computation | async-start | bytes 2097152 | tf_op jit(solution)/shard_map/all_to_all | solution.py:217
  28.2 0.0 copy-done.13
  28.2 0.2 copy.13
  28.4 0.0 copy-done.6
  28.4 0.0 copy-done.7
  28.5 0.0 copy-done.8
  28.5 0.0 copy-done.9
  28.5 0.0 copy-start.10
  28.5 0.0 copy-start.11
  28.5 0.0 copy-start.12
  28.5 5.6 %filter.1.filt_ref = f32[32,128,256]{2,1,0:T(8,128)S(1)} custom-call(bf16[32,128,128]{2,1,0:T(8,128)(2,1)S(1)} %bitcast.7, f32[1,32]{1,0:T(1,128)S(1)} %copy-done.9, bf16[256,256]{1,0:T(8,128)(2,1)S(1)} %copy-done.8, f32[2,128,128]{2,1,0:T(8,128)S(1)} %copy-done.7, bf16[768,256]{1,0:T(8,128)(2,1)S(1)} %copy-done.6), custom_call_target="tpu_custom_call" | custom-call | flops 1073741824 | bytes 5242880 | tf_op jit(solution)/shard_map/filter/pallas_call | solution.py:238
  34.2 0.0 copy-start.4
  34.2 1.9 %copy-done.4 = f32[32,128,256]{2,1,0:T(8,128)} copy-done((f32[32,128,256]{2,1,0:T(8,128)}, f32[32,128,256]{2,1,0:T(8,128)S(1)}, u32[]{:S(2)}) %copy-start.4) | copy-done | bytes 4194328
  36.1 9.0 %all-to-all-done.x_ref = bf16[64,32,256]{2,1,0:T(8,128)(2,1)S(1)} async-done(((bf16[64,32,256]{2,1,0:T(8,128)(2,1)}), bf16[64,32,256]{2,1,0:T(8,128)(2,1)S(1)}, u32[]{:S(2)}, u32[]{:S(2)}) %all-to-all-start) | async-done | bytes 1048608 | tf_op jit(solution)/shard_map/all_to_all | solution.py:217
  45.1 0.0 copy-done.10
  45.1 0.0 copy-done.11
  45.1 0.0 copy-done.12
  45.1 14.7 %long.1 = bf16[64,32,256]{2,1,0:T(8,128)(2,1)} custom-call(bf16[64,32,256]{2,1,0:T(8,128)(2,1)S(1)} %all-to-all-done.x_ref, f32[32,128,256]{2,1,0:T(8,128)} %copy-done.4, bf16[256,256]{1,0:T(8,128)(2,1)S(1)} %copy-done.12, f32[2,128,128]{2,1,0:T(8,128)S(1)} %copy-done.7, bf16[768,256]{1,0:T(8,128)(2,1)S(1)} %copy-done.6, bf16[768,256]{1,0:T(8,128)(2,1)S(1)} %copy-done.10, ...), custom_call_target="tpu_custom_call" | custom-call | flops 2147483648 | bytes 7340032 | tf_op jit(solution)/shard_map/long/pallas_call | solution.py:257
  59.8 5.4 %all-to-all-start.1 = ((bf16[64,32,256]{2,1,0:T(8,128)(2,1)}), bf16[64,32,256]{2,1,0:T(8,128)(2,1)S(1)}, u32[]{:S(2)}, u32[]{:S(2)}) async-start(bf16[64,32,256]{2,1,0:T(8,128)(2,1)} %long.1), calls=%async_computation.1 | async-start | bytes 2097152 | tf_op jit(solution)/shard_map/all_to_all | solution.py:269
  65.2 0.0 copy-done.1
  65.3 3.2 %query.1 = bf16[2048,256]{1,0:T(8,128)(2,1)S(1)} custom-call(bf16[2048,256]{1,0:T(8,128)(2,1)S(1)} %copy-done.1, bf16[32,2048]{1,0:T(8,128)(2,1)S(1)} %collective-permute-done.halo_ref, f32[3,7,2048]{2,1,0:T(8,128)S(1)} %copy-done.5), custom_call_target="tpu_custom_call" | custom-call | flops 7864320 | bytes 2097152 | tf_op jit(solution)/shard_map/query/pallas_call | solution.py:221
  68.5 13.7 %all-to-all-done.1 = bf16[64,32,256]{2,1,0:T(8,128)(2,1)S(1)} async-done(((bf16[64,32,256]{2,1,0:T(8,128)(2,1)}), bf16[64,32,256]{2,1,0:T(8,128)(2,1)S(1)}, u32[]{:S(2)}, u32[]{:S(2)}) %all-to-all-start.1) | async-done | bytes 1048608 | tf_op jit(solution)/shard_map/all_to_all | solution.py:269
  82.2 1.3 %fusion = bf16[2048,256]{1,0:T(8,128)(2,1)} fusion(bf16[2048,256]{1,0:T(8,128)(2,1)S(1)} %query.1, bf16[64,32,256]{2,1,0:T(8,128)(2,1)S(1)} %all-to-all-done.1), kind=kLoop, calls=%fused_computation.1 | loop fusion | flops 2097152 | bytes 3145728 | tf_op jit(solution)/shard_map/convert_element_type | solution.py:271
  (9 shorter events, 0.0 us)
Async XLA Ops:
  0.0 1.2 %copy-start = (bf16[2048,256]{1,0:T(8,128)(2,1)S(1)}, bf16[2048,256]{1,0:T(8,128)(2,1)}, u32[]{:S(2)}) copy-start(bf16[2048,256]{1,0:T(8,128)(2,1)} %q_ref.3) | copy-start | bytes 3145732
  1.2 1.2 %copy-start.2 = (bf16[2048,256]{1,0:T(8,128)(2,1)S(1)}, bf16[2048,256]{1,0:T(8,128)(2,1)}, u32[]{:S(2)}) copy-start(bf16[2048,256]{1,0:T(8,128)(2,1)} %k_ref.3) | copy-start | bytes 3145732
  2.5 1.2 %copy-start.3 = (bf16[2048,256]{1,0:T(8,128)(2,1)S(1)}, bf16[2048,256]{1,0:T(8,128)(2,1)}, u32[]{:S(2)}) copy-start(bf16[2048,256]{1,0:T(8,128)(2,1)} %v_ref.3) | copy-start | bytes 3145732
  3.7 7.6 %copy-start.5 = (f32[3,7,2048]{2,1,0:T(8,128)S(1)}, f32[3,7,2048]{2,1,0:T(8,128)}, u32[]{:S(2)}) copy-start(f32[3,7,2048]{2,1,0:T(8,128)} %taps_ref.3) | copy-start | bytes 516100
  4.7 23.5 %copy-start.13 = (bf16[1,32,16384]{2,1,0:T(8,128)(2,1)S(1)}, bf16[1,32,16384]{2,1,0:T(8,128)(2,1)}, u32[]{:S(2)}) copy-start(bf16[1,32,16384]{2,1,0:T(8,128)(2,1)} %param.16) | copy-start | bytes 3145732
  4.7 6.6 %collective-permute-start = (bf16[32,2048]{1,0:T(8,128)(2,1)S(1)}, bf16[32,2048]{1,0:T(8,128)(2,1)S(1)}, u32[]{:S(2)}, u32[]{:S(2)}) collective-permute-start(bf16[32,2048]{1,0:T(8,128)(2,1)S(1)} %tail.1), channel_id=1, source_target_pairs={{0,4},{4,8},{8,12},{12,16},{16,20},{20,24},{24,28},{28,32},{32,36}... | collective-permute-start | bytes 393224 | tf_op jit(solution)/shard_map/ppermute | solution.py:197
  17.8 10.6 %copy-start.6 = (bf16[768,256]{1,0:T(8,128)(2,1)S(1)}, bf16[768,256]{1,0:T(8,128)(2,1)}, u32[]{:S(2)}) copy-start(bf16[768,256]{1,0:T(8,128)(2,1)} %constant.15.clone.ahead_ref) | copy-start | bytes 1179652
  17.8 10.6 %copy-start.7 = (f32[2,128,128]{2,1,0:T(8,128)S(1)}, f32[2,128,128]{2,1,0:T(8,128)}, u32[]{:S(2)}) copy-start(f32[2,128,128]{2,1,0:T(8,128)} %constant.14.clone.twist_ref) | copy-start | bytes 393220
  17.8 10.6 %copy-start.8 = (bf16[256,256]{1,0:T(8,128)(2,1)S(1)}, bf16[256,256]{1,0:T(8,128)(2,1)}, u32[]{:S(2)}) copy-start(bf16[256,256]{1,0:T(8,128)(2,1)} %constant.12.clone.first_ref) | copy-start | bytes 393220
  17.8 10.6 %copy-start.9 = (f32[1,32]{1,0:T(1,128)S(1)}, f32[1,32]{1,0:T(1,128)}, u32[]{:S(2)}) copy-start(f32[1,32]{1,0:T(1,128)} %gain_ref.1) | copy-start | bytes 388
  17.8 27.3 %all-to-all-start = ((bf16[64,32,256]{2,1,0:T(8,128)(2,1)}), bf16[64,32,256]{2,1,0:T(8,128)(2,1)S(1)}, u32[]{:S(2)}, u32[]{:S(2)}) async-start(bf16[64,32,256]{2,1,0:T(8,128)(2,1)} %bitcast), calls=%async_computation | async-start | bytes 2097152 | tf_op jit(solution)/shard_map/all_to_all | solution.py:217
  28.5 16.6 %copy-start.10 = (bf16[768,256]{1,0:T(8,128)(2,1)S(1)}, bf16[768,256]{1,0:T(8,128)(2,1)}, u32[]{:S(2)}) copy-start(bf16[768,256]{1,0:T(8,128)(2,1)} %constant.16.clone.back_ref) | copy-start | bytes 1179652
  28.5 16.6 %copy-start.11 = (bf16[128,768]{1,0:T(8,128)(2,1)S(1)}, bf16[128,768]{1,0:T(8,128)(2,1)}, u32[]{:S(2)}) copy-start(bf16[128,768]{1,0:T(8,128)(2,1)} %constant.17.clone.last_ref) | copy-start | bytes 589828
  28.5 16.6 %copy-start.12 = (bf16[256,256]{1,0:T(8,128)(2,1)S(1)}, bf16[256,256]{1,0:T(8,128)(2,1)}, u32[]{:S(2)}) copy-start(bf16[256,256]{1,0:T(8,128)(2,1)} %constant.13.clone.first_ref) | copy-start | bytes 393220
  34.2 2.0 %copy-start.4 = (f32[32,128,256]{2,1,0:T(8,128)}, f32[32,128,256]{2,1,0:T(8,128)S(1)}, u32[]{:S(2)}) copy-start(f32[32,128,256]{2,1,0:T(8,128)S(1)} %filter.1.filt_ref) | copy-start | bytes 12582916
  59.8 5.5 %copy-start.1 = (bf16[2048,256]{1,0:T(8,128)(2,1)S(1)}, bf16[2048,256]{1,0:T(8,128)(2,1)}, u32[]{:S(2)}) copy-start(bf16[2048,256]{1,0:T(8,128)(2,1)} %q_ref.3) | copy-start | bytes 3145732
  59.8 22.4 %all-to-all-start.1 = ((bf16[64,32,256]{2,1,0:T(8,128)(2,1)}), bf16[64,32,256]{2,1,0:T(8,128)(2,1)S(1)}, u32[]{:S(2)}, u32[]{:S(2)}) async-start(bf16[64,32,256]{2,1,0:T(8,128)(2,1)} %long.1), calls=%async_computation.1 | async-start | bytes 2097152 | tf_op jit(solution)/shard_map/all_to_all | solution.py:269
where the time goes:
time: 83.9 us; the launch traced here: 83.5 us
  Pallas kernels  31.1 us (37%)
  waiting for transfers between devices  24.6 us (29%)
  starting transfers between devices  20.4 us (24%)
  local copies, waits for them, and re-layouts  5.91 us (7%)
  other arithmetic  1.3 us (2%)
    pallas_call x1, Pallas kernels, local(): pl.pallas_call(long_kernel, grid=(owned // count,), in_specs=[whole, spec...  14.7 us
    all_to_all x1, waiting for transfers between devices, local(): lax.all_to_all(long, 'ctx', split_axis=0, concat_axis=0, tiled=True)  13.7 us
    all_to_all x1, starting transfers between devices, local(): lax.all_to_all(gated.reshape(ctx_count, owned, tokens), 'ctx', split_axis...  10.3 us
    all_to_all x1, waiting for transfers between devices, local(): lax.all_to_all(gated.reshape(ctx_count, owned, tokens), 'ctx', split_axis...  8.99 us
    pallas_call x1, Pallas kernels, local(): pl.pallas_call(gate_kernel, grid=(width // rows,), in_specs=[data_spec, d...  6.52 us
    unnamed x29, local copies, waits for them, and re-layouts  5.91 us
    pallas_call x1, Pallas kernels, local(): pl.pallas_call(filter_kernel, grid=(owned // count,), in_specs=[pl.BlockS...  5.64 us
    all_to_all x1, starting transfers between devices, local(): lax.all_to_all(long, 'ctx', split_axis=0, concat_axis=0, tiled=True)  5.44 us
  transfers between devices with their start and end apart: 3, of which 3 were waited for; matrix products, arithmetic and copies ran while one was open for 0% of the time, Pallas kernels for 11%

commit v1 on v0

v1 whole, which is shorter than its diff:
```python
import jax
import jax.numpy as jnp
import numpy as np
from jax import lax
from jax.experimental import pallas as pl
from jax.experimental.pallas import tpu as pltpu
from jax.sharding import PartitionSpec as P

VMEM_LIMIT = 24 * 1024 * 1024
VMEM_FILTER = 60 * 1024 * 1024
VMEM_SOME = 52 * 1024 * 1024
VMEM_MOST = 63 * 1024 * 1024
RIM = 8
TAPS = 7
GROUP = 8
BF16, F32 = jnp.bfloat16, jnp.float32


def head_and_rest(table):
    head = table.astype(np.float32).astype(jnp.bfloat16)
    rest = (table - head.astype(np.float64)).astype(np.float32).astype(jnp.bfloat16)
    return head, rest


def transform_tables(side, runs):
    length = side * side
    k = np.arange(side)
    natural = np.arange(side)
    blocks = side // runs
    held = (np.arange(blocks)[None, :] * runs + np.arange(runs)[:, None]).reshape(-1)

    def first(order):
        angle = 2 * np.pi * (k[:, None] + 0.25) * order[None, :] / side
        both = np.concatenate([np.cos(angle), np.sin(angle)], axis=0)
        return np.concatenate(head_and_rest(both), axis=1)

    turn = 2 * np.pi * (k[:, None] + 0.25) * natural[None, :] / length
    twist = np.stack([np.cos(turn), np.sin(turn)]).astype(np.float32)
    angle = 2 * np.pi * (natural[:, None] * k[None, :] % side) / side
    cos, sin = np.cos(angle), np.sin(angle)

    def second(matrix):
        head, rest = head_and_rest(matrix)
        return np.concatenate([head, head, rest], axis=0)

    ahead = second(np.block([[cos, sin], [-sin, cos]]))
    back = second(np.block([[cos, -sin], [sin, cos]]))
    angle = 2 * np.pi * held[:, None] * (k[None, :] + 0.25) / side
    head, rest = head_and_rest(np.concatenate([np.cos(angle), np.sin(angle)], axis=1) / length)
    last = np.concatenate([head, head, rest], axis=1)
    return first(natural), first(held), twist, ahead, back, last


def split(array):
    head = array.astype(BF16)
    return head, (array - head.astype(F32)).astype(BF16)


def dot(a, b):
    return jnp.dot(a, b, preferred_element_type=F32)


def fetch(source, target, sems, columns):
    rows = target.shape[0] // sems.shape[0]
    copies = []
    for i in range(sems.shape[0]):
        cut = pl.ds(i * rows, rows)
        copies.append(
            pltpu.make_async_copy(source.at[cut, columns], target.at[cut], sems.at[i])
        )
        copies[-1].start()
    return copies


def tail_kernel(q_ref, out_ref, held, sems):
    copies = fetch(q_ref, held, sems, pl.ds(q_ref.shape[1] - 128, 128))
    rows = held.shape[0] // len(copies)
    for i, copy in enumerate(copies):
        copy.wait()
        out_ref[:, i * rows : (i + 1) * rows] = held[i * rows : (i + 1) * rows].T[-2 * RIM :]


def short_conv(block, halo, taps_ref, which, c0, ext):
    count = block.shape[0]
    ext[:RIM] = halo
    ext[RIM:] = block
    channels = pl.ds(c0, 128)
    total = taps_ref[which, 0:1, channels] * block
    for j in range(1, taps_ref.shape[1]):
        total = total + taps_ref[which, j : j + 1, channels] * ext[RIM - j : RIM - j + count]
    return total


def gate_kernel(
    k_ref, v_ref, far_ref, out_ref, ext, held, done, taps_ref, sems_in, sems_out, sem_taps
):
    width, tokens = k_ref.shape
    runs = tokens // 128
    owned = width // out_ref.shape[0]
    fit = 128 // owned
    chunks = sems_out.shape[0]
    rows = width // chunks
    lane = lax.broadcasted_iota(jnp.int32, (RIM, 128), 1) // owned
    nothing = jnp.zeros((RIM, 128), F32)
    turn = lax.axis_index("ctx") % fit

    def fetch(i):
        cut = pl.ds(i * rows, rows)
        for n, ref in enumerate((k_ref, v_ref)):
            yield pltpu.make_async_copy(ref.at[cut], held.at[n, cut], sems_in.at[n, i])

    def send(i):
        cut = pl.ds(i * rows // owned, rows // owned)
        return pltpu.make_async_copy(done.at[cut], out_ref.at[cut], sems_out.at[i])

    taps_copy = pltpu.make_async_copy(far_ref, taps_ref, sem_taps)
    taps_copy.start()
    for i in range(chunks):
        for copy in fetch(i):
            copy.start()
    taps_copy.wait()
    for i in range(chunks):
        for copy in fetch(i):
            copy.wait()
        for c in range(i * rows, (i + 1) * rows, 128):
            both, rims = [], []
            for n in range(2):
                turned = held[n, c : c + 128].T.astype(F32)
                both.append(short_conv(turned, nothing, taps_ref, n + 1, c, ext.at[n]))
                rims.append((turned[tokens - RIM :], turned[:RIM]))
            gated = (both[0] * both[1]).astype(BF16)
            first = c // owned
            for j in range(runs):
                piece = gated[j * 128 : (j + 1) * 128].T
                done[first : first + fit, j * owned : (j + 1) * owned] = piece.reshape(fit, owned, 128)
            sides = (rims[0][1], rims[0][0], rims[1][1], rims[1][0])
            for d in range(fit):
                rim = nothing
                for g, side in enumerate(sides):
                    moved = pltpu.roll(side, (g - d) % fit * owned, 1)
                    rim = jnp.where(lane == g, moved, rim)
                rim = pltpu.roll(rim, turn * owned, 1)
                done[first + d, runs * owned :] = rim.astype(BF16)
        send(i).start()
    for i in range(chunks):
        send(i).wait()


def query_kernel(q_ref, halo_ref, taps_ref, out_ref, ext):
    width = q_ref.shape[0]
    for c in range(0, width, 128):
        halo = halo_ref[:, c : c + 128].astype(F32)
        turned = q_ref[c : c + 128].T.astype(F32)
        queries = short_conv(turned, halo[RIM:], taps_ref, 0, c, ext)
        out_ref[c : c + 128] = queries.astype(BF16).T


def to_spectrum(pairs, first, twist, ahead):
    side = twist.shape[1]
    cos, sin = twist[0], twist[1]
    stacked = []
    for pair in pairs:
        both = dot(first, jnp.concatenate([pair, pair], axis=0))
        for i in range(2):
            re = both[:side, i * side : (i + 1) * side]
            im = both[side:, i * side : (i + 1) * side]
            turned = jnp.concatenate([re * cos - im * sin, re * sin + im * cos], axis=1)
            head, rest = split(turned)
            stacked.append(dot(jnp.concatenate([head, rest, head], axis=1), ahead))
    return stacked


def filter_kernel(
    filt_ref, gain_ref, first_ref, twist_ref, ahead_ref, out_ref, done, sems
):
    owned, side, _ = filt_ref.shape

    def send(step):
        cut = pl.ds(step * GROUP, GROUP)
        return pltpu.make_async_copy(done.at[cut], out_ref.at[cut], sems.at[step])

    @pl.loop(0, owned // GROUP)
    def _(step):
        base = step * GROUP
        pairs = [
            jnp.concatenate([filt_ref[base + c], filt_ref[base + c + 1]], axis=1)
            for c in range(0, GROUP, 2)
        ]
        spectrum = to_spectrum(pairs, first_ref[...], twist_ref, ahead_ref[...])
        for c, rows in enumerate(spectrum):
            re, im = rows[:, :side] + gain_ref[0, base + c], rows[:, side:]
            done[base + c] = jnp.concatenate([re, im], axis=1)
        send(step).start()

    for step in range(owned // GROUP):
        send(step).wait()


def first_tokens(x_ref, taps_ref, x_wide, ext, owned):
    blocks, rows, lanes = x_ref.shape
    fit = lanes // owned
    steps = blocks // fit
    rims = x_ref[:, rows - RIM :].astype(F32)
    before = jnp.concatenate([jnp.zeros((1, RIM, lanes), F32), rims[:-1]], axis=0)
    group = lax.broadcasted_iota(jnp.int32, (RIM, lanes), 1) // owned
    for q in range(steps):
        for n in range(2):
            for start, source in ((0, before), (RIM, rims)):
                packed = source[q * fit]
                for i in range(1, fit):
                    packed = jnp.where(group == (i + 2 * n) % fit, source[q * fit + i], packed)
                ext[n, q, start : start + RIM] = packed
    sums = []
    for n in range(2):
        total = taps_ref[RIM * n : RIM * n + 1] * ext[n, :, RIM:]
        for j in range(1, TAPS):
            tap = taps_ref[RIM * n + j : RIM * n + j + 1]
            total = total + tap * ext[n, :, RIM - j : 2 * RIM - j]
        sums.append(total)
    for q in range(steps):
        gated = sums[0][q] * pltpu.roll(sums[1][q], 2 * owned, 1)
        x_wide[0, q * lanes : (q + 1) * lanes, :RIM] = gated.T.astype(BF16).astype(F32)


def long_kernel(
    x_ref, far_ref, taps_ref, first_ref, twist_ref, ahead_ref, back_ref, last_ref, out_ref,
    x_wide, y_wide, filt_ref, ext, done, sems, sems_in,
):
    blocks, owned, width = out_ref.shape
    side = filt_ref.shape[1]

    def fetched(step):
        cut = pl.ds(step * GROUP, GROUP)
        return pltpu.make_async_copy(far_ref.at[cut], filt_ref.at[cut], sems_in.at[step])

    for step in range(owned // GROUP):
        fetched(step).start()
    runs = width // side
    for j in range(runs):
        piece = x_ref[:, j * owned : (j + 1) * owned]
        x_wide[j] = piece.astype(F32).reshape(blocks * owned, side)
    first_tokens(x_ref, taps_ref, x_wide, ext, owned)
    cos, sin = twist_ref[0], twist_ref[1]

    def some(base):
        held = []
        for c in range(GROUP):
            rows = [x_wide[j, pl.ds(base + c, blocks, stride=owned), :] for j in range(runs)]
            held.append(jnp.concatenate(rows, axis=0).astype(BF16))
        pairs = [jnp.concatenate(held[c : c + 2], axis=1) for c in range(0, GROUP, 2)]
        spectrum = to_spectrum(pairs, first_ref[...], twist_ref, ahead_ref[...])
        undone = []
        for c, rows in enumerate(spectrum):
            re, im = rows[:, :side], rows[:, side:]
            both = filt_ref[base + c]
            fre, fim = both[:, :side], both[:, side:]
            head, rest = split(jnp.concatenate([re * fre - im * fim, re * fim + im * fre], axis=1))
            undone.append(dot(jnp.concatenate([head, rest, head], axis=1), back_ref[...]))
        for c in range(0, GROUP, 2):
            columns = []
            for rows in undone[c : c + 2]:
                re, im = rows[:, :side], rows[:, side:]
                turned = jnp.concatenate([re * cos + im * sin, im * cos - re * sin], axis=0)
                head, rest = split(turned)
                columns.append(jnp.concatenate([head, rest, head], axis=0))
            result = dot(last_ref[...], jnp.concatenate(columns, axis=1))
            for i in range(2):
                for j in range(runs):
                    y_wide[j, pl.ds(base + c + i, blocks, stride=owned), :] = result[
                        j * blocks : (j + 1) * blocks, i * side : (i + 1) * side
                    ]

    part = owned // sems.shape[0]
    copies = []
    for h in range(sems.shape[0]):

        @pl.loop(0, part // GROUP)
        def _(step, h=h):
            fetched(h * (part // GROUP) + step).wait()
            some(h * part + step * GROUP)

        for j in range(runs):
            whole = y_wide[j].reshape(blocks, owned, side)
            done[h, :, :, j * side : (j + 1) * side] = (
                whole[:, h * part : (h + 1) * part].astype(BF16)
            )
        copies.append(
            pltpu.make_async_copy(done.at[h], out_ref.at[:, pl.ds(h * part, part)], sems.at[h])
        )
        copies[-1].start()
    for copy in copies:
        copy.wait()


def product_kernel(q_ref, long_ref, out_ref, done, sems):
    chunks = sems.shape[0]
    rows = done.shape[0] // chunks
    copies = []
    for i in range(chunks):
        cut = pl.ds(i * rows, rows)
        done[cut] = (q_ref[cut].astype(F32) * long_ref[cut].astype(F32)).astype(BF16)
        copies.append(pltpu.make_async_copy(done.at[cut], out_ref.at[cut], sems.at[i]))
        copies[-1].start()
    for copy in copies:
        copy.wait()


def cost(flops, size):
    return pl.CostEstimate(flops=flops, bytes_accessed=size, transcendentals=0)


def params(limit=VMEM_LIMIT):
    return pltpu.CompilerParams(vmem_limit_bytes=limit)


def local(queries, keys, values, short_taps, long_filter, skip_gain):
    ctx_count = lax.axis_size("ctx")
    width, tokens = queries.shape
    owned = width // ctx_count
    side = 128
    runs = tokens // side
    first_plain, first_held, twist, ahead, back, last = (
        jnp.asarray(t) for t in transform_tables(side, runs)
    )

    far = pl.BlockSpec(memory_space=pltpu.HBM)
    whole = pl.BlockSpec(memory_space=pltpu.VMEM)
    shift = [(i, i + 1) for i in range(ctx_count - 1)]

    shape = jax.ShapeDtypeStruct((width, tokens), BF16)
    chunks = 8
    held_rows = runs * owned + RIM
    with jax.named_scope("gate"):
        gated = pl.pallas_call(
            gate_kernel,
            in_specs=[far, far, far],
            out_specs=far,
            out_shape=jax.ShapeDtypeStruct((ctx_count, held_rows, side), BF16),
            scratch_shapes=[
                pltpu.VMEM((2, RIM + tokens, 128), F32),
                pltpu.VMEM((2, width, tokens), BF16),
                pltpu.VMEM((ctx_count, held_rows, side), BF16),
                pltpu.VMEM(short_taps.shape, F32),
                pltpu.SemaphoreType.DMA((2, chunks)),
                pltpu.SemaphoreType.DMA((chunks,)),
                pltpu.SemaphoreType.DMA,
            ],
            compiler_params=params(VMEM_MOST),
            cost_estimate=cost(30 * width * tokens, 6 * width * tokens),
        )(keys, values, short_taps)
    arrived = lax.all_to_all(gated, "ctx", split_axis=0, concat_axis=0, tiled=True)
    own_taps = lax.dynamic_slice_in_dim(short_taps, lax.axis_index("ctx") * owned, owned, 2)
    own_taps = jnp.pad(own_taps[1:], ((0, 0), (0, RIM - TAPS), (0, 0))).reshape(2 * RIM, owned)
    own_taps = jnp.tile(own_taps, (1, side // owned))
    later_queries, _ = lax.optimization_barrier((queries, gated))
    with jax.named_scope("query_tail"):
        query_tail = pl.pallas_call(
            tail_kernel,
            in_specs=[far],
            out_specs=whole,
            out_shape=jax.ShapeDtypeStruct((2 * RIM, width), BF16),
            scratch_shapes=[pltpu.VMEM((width, 128), BF16), pltpu.SemaphoreType.DMA((4,))],
            compiler_params=params(),
            cost_estimate=cost(width * 128, 2 * width * 128),
        )(later_queries)
    query_halo = lax.ppermute(query_tail, "ctx", shift)
    with jax.named_scope("filter"):
        spectrum = pl.pallas_call(
            filter_kernel,
            in_specs=[whole, pl.BlockSpec(memory_space=pltpu.SMEM), whole, whole, whole],
            out_specs=far,
            out_shape=jax.ShapeDtypeStruct((owned, side, 2 * side), F32),
            scratch_shapes=[
                pltpu.VMEM((owned, side, 2 * side), F32),
                pltpu.SemaphoreType.DMA((owned // GROUP,)),
            ],
            compiler_params=params(VMEM_FILTER),
            cost_estimate=cost(owned * side**3 * 16, 5 << 20),
        )(long_filter.reshape(owned, side, side), skip_gain, first_plain, twist, ahead)
    spectrum, query_halo = lax.optimization_barrier((spectrum, query_halo))
    with jax.named_scope("query"):
        q_short = pl.pallas_call(
            query_kernel,
            in_specs=[whole] * 3,
            out_specs=whole,
            out_shape=shape,
            scratch_shapes=[pltpu.VMEM((RIM + tokens, 128), F32)],
            compiler_params=params(),
            cost_estimate=cost(15 * width * tokens, 4 * width * tokens),
        )(later_queries, query_halo, short_taps)
    wide = pltpu.VMEM((runs, ctx_count * owned, side), F32)
    parts = 2
    with jax.named_scope("long"):
        long = pl.pallas_call(
            long_kernel,
            in_specs=[whole, far] + [whole] * 6,
            out_specs=far,
            out_shape=jax.ShapeDtypeStruct((ctx_count, owned, tokens), BF16),
            scratch_shapes=[
                wide,
                wide,
                pltpu.VMEM((owned, side, 2 * side), F32),
                pltpu.VMEM((2, ctx_count * owned // side, 2 * RIM, side), F32),
                pltpu.VMEM((parts, ctx_count, owned // parts, tokens), BF16),
                pltpu.SemaphoreType.DMA((parts,)),
                pltpu.SemaphoreType.DMA((owned // GROUP,)),
            ],
            compiler_params=params(VMEM_SOME),
            cost_estimate=cost(owned * side**3 * 32, 7 << 20),
        )(arrived, spectrum, own_taps, first_held, twist, ahead, back, last)
    returned = lax.all_to_all(long, "ctx", split_axis=0, concat_axis=0, tiled=True)
    returned = returned.reshape(width, tokens)
    with jax.named_scope("product"):
        return pl.pallas_call(
            product_kernel,
            in_specs=[whole, whole],
            out_specs=far,
            out_shape=shape,
            scratch_shapes=[pltpu.VMEM((width, tokens), BF16), pltpu.SemaphoreType.DMA((8,))],
            compiler_params=params(),
            cost_estimate=cost(width * tokens, 6 * width * tokens),
        )(q_short, returned)


def solution(mesh):
    placed = (
        P("ch", "ctx"),
        P("ch", "ctx"),
        P("ch", "ctx"),
        P(None, None, "ch"),
        P("ch", "ctx", None),
        P("ch", "ctx"),
    )
    return jax.shard_map(
        local, mesh=mesh, in_specs=placed, out_specs=P("ch", "ctx"), check_vma=False
    )
```

time: 83.9 us -> 72.8 us (0.87)
  local copies, waits for them, and re-layouts: 5.91 us -> 1.43 us
  waiting for transfers between devices: 24.6 us -> 20.2 us
  other arithmetic: 1.3 us -> 0 us
  starting transfers between devices: 20.4 us -> 19.5 us
    unnamed x29 -> x17, local copies, waits for them, and re-layouts: 5.91 us -> 1.25 us
    all_to_all x1, waiting for transfers between devices: 8.99 us -> 5.1 us  [local(): lax.all_to_all(gated, 'ctx', split_axis=0, concat_axis=0, tiled=True)]
    ppermute x1, waiting for transfers between devices: 1.93 us -> 0.05 us  [local(): query_halo = lax.ppermute(query_tail, 'ctx', shift)]
    all_to_all x1, waiting for transfers between devices: 13.7 us -> 15 us  [local(): lax.all_to_all(long, 'ctx', split_axis=0, concat_axis=0, tiled=True)]
    convert_element_type x1 -> x0, other arithmetic: 1.3 us -> none  [local(): return (q_short.astype(F32) * returned.astype(F32)).astype(BF16)]
    ppermute x1, starting transfers between devices: 4.64 us -> 3.54 us  [local(): query_halo = lax.ppermute(query_tail, 'ctx', shift)]
    pallas_call x5 -> x6, Pallas kernels: 31.1 us -> 31.2 us  [the longest x1 13.6 us: local(): pl.pallas_call(long_kernel, in_specs=[whole, far] + [whole] * 6, out_spec...]
  transfers between devices with their start and end apart: 3 -> 3, of which waited for: 3 -> 3; matrix products, arithmetic and copies ran while one was open for 0% -> 2% of each run, Pallas kernels for 11% -> 14%
where the time goes in v1:
time: 72.8 us; the launch traced here: 72.5 us
  Pallas kernels  31.2 us (43%)
  waiting for transfers between devices  20.2 us (28%)
  starting transfers between devices  19.5 us (27%)
  local copies, waits for them, and re-layouts  1.43 us (2%)
    all_to_all x1, waiting for transfers between devices, local(): lax.all_to_all(long, 'ctx', split_axis=0, concat_axis=0, tiled=True)  15 us
    pallas_call x1, Pallas kernels, local(): pl.pallas_call(long_kernel, in_specs=[whole, far] + [whole] * 6, out_spec...  13.6 us
    all_to_all x1, starting transfers between devices, local(): lax.all_to_all(gated, 'ctx', split_axis=0, concat_axis=0, tiled=True)  10.7 us
    pallas_call x1, Pallas kernels, local(): pl.pallas_call(filter_kernel, in_specs=[whole, pl.BlockSpec(memory_space=...  7.81 us
    pallas_call x1, Pallas kernels, local(): pl.pallas_call(gate_kernel, in_specs=[far, far, far], out_specs=far, out_...  6.4 us
    all_to_all x1, starting transfers between devices, local(): lax.all_to_all(long, 'ctx', split_axis=0, concat_axis=0, tiled=True)  5.29 us
    all_to_all x1, waiting for transfers between devices, local(): lax.all_to_all(gated, 'ctx', split_axis=0, concat_axis=0, tiled=True)  5.1 us
    ppermute x1, starting transfers between devices, local(): query_halo = lax.ppermute(query_tail, 'ctx', shift)  3.54 us
  transfers between devices with their start and end apart: 3, of which 3 were waited for; matrix products, arithmetic and copies ran while one was open for 2% of the time, Pallas kernels for 14%

profile of v1, /device:TPU:1, one launch (start us, length us, event | category | flops | bytes accessed | tf_op | source)
XLA Modules:
  0.0 72.5 jit_solution(4964823778562399472)
XLA Ops:
  0.0 6.4 %gate.1 = bf16[64,72,128]{2,1,0:T(8,128)(2,1)} custom-call(bf16[2048,256]{1,0:T(8,128)(2,1)} %k_ref.1, bf16[2048,256]{1,0:T(8,128)(2,1)} %v_ref.1, f32[3,7,2048]{2,1,0:T(8,128)} %taps_ref.1), custom_call_target="tpu_custom_call" | custom-call | flops 15728640 | bytes 3145728 | tf_op jit(solution)/shard_map/gate/pallas_call | solution.py:334
  6.4 0.0 copy-start
  6.4 0.0 copy-start.1
  6.4 10.7 %all-to-all-start = ((bf16[64,72,128]{2,1,0:T(8,128)(2,1)}), bf16[64,72,128]{2,1,0:T(8,128)(2,1)}, u32[]{:S(2)}, u32[]{:S(2)}) async-start(bf16[64,72,128]{2,1,0:T(8,128)(2,1)} %gate.1), calls=%async_computation | async-start | bytes 2359296 | tf_op jit(solution)/shard_map/all_to_all | solution.py:351
  17.1 0.0 copy-done
  17.1 0.0 copy-start.7
  17.1 0.5 query_tail.1
  17.6 3.5 %collective-permute-start = (bf16[16,2048]{1,0:T(8,128)(2,1)S(1)}, bf16[16,2048]{1,0:T(8,128)(2,1)S(1)}, u32[]{:S(2)}, u32[]{:S(2)}) collective-permute-start(bf16[16,2048]{1,0:T(8,128)(2,1)S(1)} %query_tail.1), channel_id=1, source_target_pairs={{0,4},{4,8},{8,12},{12,16},{16,20},{20,24},{24,28},{28,32},{32,36}... | collective-permute-start | bytes 196616 | tf_op jit(solution)/shard_map/ppermute | solution.py:366
  21.2 0.0 copy-done.1
  21.2 0.1 constant_dynamic-slice_fusion
  21.3 0.1 tile.12.taps_ref
  21.4 0.0 copy-done.7
  21.4 1.2 %copy.13 = bf16[4,8,128,128]{3,2,1,0:T(8,128)(2,1)} copy(bf16[4,8,128,128]{3,1,2,0:T(8,128)(2,1)S(1)} %bitcast.8) | data formatting | bytes 2097152
  22.6 0.0 copy-start.2
  22.6 0.0 copy-start.3
  22.6 0.0 copy-start.4
  22.6 0.0 copy-start.5
  22.6 0.0 copy-start.6
  22.6 7.8 %filter.1.far_ref = f32[32,128,256]{2,1,0:T(8,128)} custom-call(bf16[32,128,128]{2,1,0:T(8,128)(2,1)} %bitcast.7, f32[1,32]{1,0:T(1,128)} %gain_ref.1, bf16[256,256]{1,0:T(8,128)(2,1)} %constant.26.clone.first_ref, f32[2,128,128]{2,1,0:T(8,128)} %constant.28.clone.twist_ref, bf16[768,256]{1,0:T(8,128)(2,1)} %constant.29.clone.ahead_ref), custom_call_target="tpu_custom_call" | custom-call | flops 1073741824 | bytes 5242880 | tf_op jit(solution)/shard_map/filter/pallas_call | solution.py:368
  30.4 0.1 collective-permute-done.halo_ref
  30.5 5.1 %all-to-all-done.x_ref = bf16[64,72,128]{2,1,0:T(8,128)(2,1)} async-done(((bf16[64,72,128]{2,1,0:T(8,128)(2,1)}), bf16[64,72,128]{2,1,0:T(8,128)(2,1)}, u32[]{:S(2)}, u32[]{:S(2)}) %all-to-all-start) | async-done | bytes 1179680 | tf_op jit(solution)/shard_map/all_to_all | solution.py:351
  35.6 0.0 copy-done.2
  35.6 0.0 copy-done.3
  35.6 0.0 copy-done.4
  35.6 0.0 copy-done.5
  35.6 0.0 copy-done.6
  35.6 13.6 %long.1 = bf16[64,32,256]{2,1,0:T(8,128)(2,1)} custom-call(bf16[64,72,128]{2,1,0:T(8,128)(2,1)} %all-to-all-done.x_ref, f32[32,128,256]{2,1,0:T(8,128)} %filter.1.far_ref, f32[16,128]{1,0:T(8,128)S(1)} %tile.12.taps_ref, bf16[256,256]{1,0:T(8,128)(2,1)S(1)} %copy-done.6, f32[2,128,128]{2,1,0:T(8,128)S(1)} %copy-done.3, bf16[768,256]{1,0:T(8,128)(2,1)S(1)} %copy-done.2, ...), custom_call_target="tpu_custom_call" | custom-call | flops 2147483648 | bytes 7340032 | tf_op jit(solution)/shard_map/long/pallas_call | solution.py:394
  49.2 5.3 %all-to-all-start.1 = ((bf16[64,32,256]{2,1,0:T(8,128)(2,1)}), bf16[64,32,256]{2,1,0:T(8,128)(2,1)S(1)}, u32[]{:S(2)}, u32[]{:S(2)}) async-start(bf16[64,32,256]{2,1,0:T(8,128)(2,1)} %long.1), calls=%async_computation.1 | async-start | bytes 2097152 | tf_op jit(solution)/shard_map/all_to_all | solution.py:411
  54.5 1.9 %query.1.q_ref = bf16[2048,256]{1,0:T(8,128)(2,1)S(1)} custom-call(bf16[2048,256]{1,0:T(8,128)(2,1)S(1)} %copy-done, bf16[16,2048]{1,0:T(8,128)(2,1)S(1)} %collective-permute-done.halo_ref, f32[3,7,2048]{2,1,0:T(8,128)S(1)} %copy-done.1), custom_call_target="tpu_custom_call" | custom-call | flops 7864320 | bytes 2097152 | tf_op jit(solution)/shard_map/query/pallas_call | solution.py:382
  56.4 15.0 %all-to-all-done.1 = bf16[64,32,256]{2,1,0:T(8,128)(2,1)S(1)} async-done(((bf16[64,32,256]{2,1,0:T(8,128)(2,1)}), bf16[64,32,256]{2,1,0:T(8,128)(2,1)S(1)}, u32[]{:S(2)}, u32[]{:S(2)}) %all-to-all-start.1) | async-done | bytes 1048608 | tf_op jit(solution)/shard_map/all_to_all | solution.py:411
  71.4 1.1 %product.1 = bf16[2048,256]{1,0:T(8,128)(2,1)} custom-call(bf16[2048,256]{1,0:T(8,128)(2,1)S(1)} %query.1.q_ref, bf16[2048,256]{1,0:T(8,128)(2,1)S(1)} %bitcast.6), custom_call_target="tpu_custom_call" | custom-call | flops 524288 | bytes 3145728 | tf_op jit(solution)/shard_map/product/pallas_call | solution.py:414
  (2 shorter events, 0.0 us)
Async XLA Ops:
  6.4 10.7 %copy-start = (bf16[2048,256]{1,0:T(8,128)(2,1)S(1)}, bf16[2048,256]{1,0:T(8,128)(2,1)}, u32[]{:S(2)}) copy-start(bf16[2048,256]{1,0:T(8,128)(2,1)} %q_ref.1) | copy-start | bytes 3145732
  6.4 14.7 %copy-start.1 = (f32[3,7,2048]{2,1,0:T(8,128)S(1)}, f32[3,7,2048]{2,1,0:T(8,128)}, u32[]{:S(2)}) copy-start(f32[3,7,2048]{2,1,0:T(8,128)} %taps_ref.1) | copy-start | bytes 516100
  6.4 29.1 %all-to-all-start = ((bf16[64,72,128]{2,1,0:T(8,128)(2,1)}), bf16[64,72,128]{2,1,0:T(8,128)(2,1)}, u32[]{:S(2)}, u32[]{:S(2)}) async-start(bf16[64,72,128]{2,1,0:T(8,128)(2,1)} %gate.1), calls=%async_computation | async-start | bytes 2359296 | tf_op jit(solution)/shard_map/all_to_all | solution.py:351
  17.1 4.2 %copy-start.7 = (bf16[1,32,16384]{2,1,0:T(8,128)(2,1)S(1)}, bf16[1,32,16384]{2,1,0:T(8,128)(2,1)}, u32[]{:S(2)}) copy-start(bf16[1,32,16384]{2,1,0:T(8,128)(2,1)} %param.16) | copy-start | bytes 3145732
  17.6 12.8 %collective-permute-start = (bf16[16,2048]{1,0:T(8,128)(2,1)S(1)}, bf16[16,2048]{1,0:T(8,128)(2,1)S(1)}, u32[]{:S(2)}, u32[]{:S(2)}) collective-permute-start(bf16[16,2048]{1,0:T(8,128)(2,1)S(1)} %query_tail.1), channel_id=1, source_target_pairs={{0,4},{4,8},{8,12},{12,16},{16,20},{20,24},{24,28},{28,32},{32,36}... | collective-permute-start | bytes 196616 | tf_op jit(solution)/shard_map/ppermute | solution.py:366
  22.6 13.0 %copy-start.2 = (bf16[768,256]{1,0:T(8,128)(2,1)S(1)}, bf16[768,256]{1,0:T(8,128)(2,1)}, u32[]{:S(2)}) copy-start(bf16[768,256]{1,0:T(8,128)(2,1)} %constant.29.clone.ahead_ref) | copy-start | bytes 1179652
  22.6 13.0 %copy-start.3 = (f32[2,128,128]{2,1,0:T(8,128)S(1)}, f32[2,128,128]{2,1,0:T(8,128)}, u32[]{:S(2)}) copy-start(f32[2,128,128]{2,1,0:T(8,128)} %constant.28.clone.twist_ref) | copy-start | bytes 393220
  22.6 13.0 %copy-start.4 = (bf16[768,256]{1,0:T(8,128)(2,1)S(1)}, bf16[768,256]{1,0:T(8,128)(2,1)}, u32[]{:S(2)}) copy-start(bf16[768,256]{1,0:T(8,128)(2,1)} %constant.30.clone.back_ref) | copy-start | bytes 1179652
  22.6 13.0 %copy-start.5 = (bf16[128,768]{1,0:T(8,128)(2,1)S(1)}, bf16[128,768]{1,0:T(8,128)(2,1)}, u32[]{:S(2)}) copy-start(bf16[128,768]{1,0:T(8,128)(2,1)} %constant.31.clone.last_ref) | copy-start | bytes 589828
  22.6 13.0 %copy-start.6 = (bf16[256,256]{1,0:T(8,128)(2,1)S(1)}, bf16[256,256]{1,0:T(8,128)(2,1)}, u32[]{:S(2)}) copy-start(bf16[256,256]{1,0:T(8,128)(2,1)} %constant.27.clone.first_ref) | copy-start | bytes 393220
  49.2 22.2 %all-to-all-start.1 = ((bf16[64,32,256]{2,1,0:T(8,128)(2,1)}), bf16[64,32,256]{2,1,0:T(8,128)(2,1)S(1)}, u32[]{:S(2)}, u32[]{:S(2)}) async-start(bf16[64,32,256]{2,1,0:T(8,128)(2,1)} %long.1), calls=%async_computation.1 | async-start | bytes 2097152 | tf_op jit(solution)/shard_map/all_to_all | solution.py:411

commit v2 on v1

--- a/solution.py
+++ b/solution.py
@@ -12,7 +12,8 @@
 VMEM_MOST = 63 * 1024 * 1024
 RIM = 8
 TAPS = 7
-GROUP = 8
+GROUP = 16
+PIECE = 8
 BF16, F32 = jnp.bfloat16, jnp.float32
 
 
@@ -126,7 +127,8 @@
             both, rims = [], []
             for n in range(2):
                 turned = held[n, c : c + 128].T.astype(F32)
-                both.append(short_conv(turned, nothing, taps_ref, n + 1, c, ext.at[n]))
+                rows_ext = ext.at[c // 128 % ext.shape[0], n]
+                both.append(short_conv(turned, nothing, taps_ref, n + 1, c, rows_ext))
                 rims.append((turned[tokens - RIM :], turned[:RIM]))
             gated = (both[0] * both[1]).astype(BF16)
             first = c // owned
@@ -155,19 +157,23 @@
         out_ref[c : c + 128] = queries.astype(BF16).T
 
 
+def enter_pair(pair, first, cos, sin):
+    side = pair.shape[0]
+    both = dot(first, jnp.concatenate([pair, pair], axis=0))
+    parts = []
+    for i in range(2):
+        re = both[:side, i * side : (i + 1) * side]
+        im = both[side:, i * side : (i + 1) * side]
+        turned = jnp.concatenate([re * cos - im * sin, re * sin + im * cos], axis=1)
+        head, rest = split(turned)
+        parts.append(jnp.concatenate([head, rest, head], axis=1))
+    return parts
+
+
 def to_spectrum(pairs, first, twist, ahead):
-    side = twist.shape[1]
-    cos, sin = twist[0], twist[1]
-    stacked = []
-    for pair in pairs:
-        both = dot(first, jnp.concatenate([pair, pair], axis=0))
-        for i in range(2):
-            re = both[:side, i * side : (i + 1) * side]
-            im = both[side:, i * side : (i + 1) * side]
-            turned = jnp.concatenate([re * cos - im * sin, re * sin + im * cos], axis=1)
-            head, rest = split(turned)
-            stacked.append(dot(jnp.concatenate([head, rest, head], axis=1), ahead))
-    return stacked
+    return [
+        dot(part, ahead) for pair in pairs for part in enter_pair(pair, first, twist[0], twist[1])
+    ]
 
 
 def filter_kernel(
@@ -176,15 +182,15 @@
     owned, side, _ = filt_ref.shape
 
     def send(step):
-        cut = pl.ds(step * GROUP, GROUP)
+        cut = pl.ds(step * PIECE, PIECE)
         return pltpu.make_async_copy(done.at[cut], out_ref.at[cut], sems.at[step])
 
-    @pl.loop(0, owned // GROUP)
+    @pl.loop(0, owned // PIECE)
     def _(step):
-        base = step * GROUP
+        base = step * PIECE
         pairs = [
             jnp.concatenate([filt_ref[base + c], filt_ref[base + c + 1]], axis=1)
-            for c in range(0, GROUP, 2)
+            for c in range(0, PIECE, 2)
         ]
         spectrum = to_spectrum(pairs, first_ref[...], twist_ref, ahead_ref[...])
         for c, rows in enumerate(spectrum):
@@ -192,7 +198,7 @@
             done[base + c] = jnp.concatenate([re, im], axis=1)
         send(step).start()
 
-    for step in range(owned // GROUP):
+    for step in range(owned // PIECE):
         send(step).wait()
 
 
@@ -223,71 +229,101 @@
 
 
 def long_kernel(
-    x_ref, far_ref, taps_ref, first_ref, twist_ref, ahead_ref, back_ref, last_ref, out_ref,
-    x_wide, y_wide, filt_ref, ext, done, sems, sems_in,
+    x_ref, far_ref, far_taps_ref, first_ref, twist_ref, ahead_ref, back_ref, last_ref, out_ref,
+    x_wide, y_wide, filt_ref, taps_ref, ext, done, sems, sems_in, sem_taps,
 ):
     blocks, owned, width = out_ref.shape
     side = filt_ref.shape[1]
 
-    def fetched(step):
-        cut = pl.ds(step * GROUP, GROUP)
-        return pltpu.make_async_copy(far_ref.at[cut], filt_ref.at[cut], sems_in.at[step])
-
-    for step in range(owned // GROUP):
-        fetched(step).start()
+    def fetched(piece):
+        cut = pl.ds(piece * PIECE, PIECE)
+        return pltpu.make_async_copy(far_ref.at[cut], filt_ref.at[cut], sems_in.at[piece])
+
+    taps_copy = pltpu.make_async_copy(far_taps_ref, taps_ref, sem_taps)
+    taps_copy.start()
+    fetched(0).start()
     runs = width // side
     for j in range(runs):
         piece = x_ref[:, j * owned : (j + 1) * owned]
         x_wide[j] = piece.astype(F32).reshape(blocks * owned, side)
+    taps_copy.wait()
     first_tokens(x_ref, taps_ref, x_wide, ext, owned)
     cos, sin = twist_ref[0], twist_ref[1]
 
     def some(base):
-        held = []
-        for c in range(GROUP):
-            rows = [x_wide[j, pl.ds(base + c, blocks, stride=owned), :] for j in range(runs)]
-            held.append(jnp.concatenate(rows, axis=0).astype(BF16))
-        pairs = [jnp.concatenate(held[c : c + 2], axis=1) for c in range(0, GROUP, 2)]
-        spectrum = to_spectrum(pairs, first_ref[...], twist_ref, ahead_ref[...])
-        undone = []
-        for c, rows in enumerate(spectrum):
-            re, im = rows[:, :side], rows[:, side:]
-            both = filt_ref[base + c]
-            fre, fim = both[:, :side], both[:, side:]
-            head, rest = split(jnp.concatenate([re * fre - im * fim, re * fim + im * fre], axis=1))
-            undone.append(dot(jnp.concatenate([head, rest, head], axis=1), back_ref[...]))
-        for c in range(0, GROUP, 2):
-            columns = []
-            for rows in undone[c : c + 2]:
+        first, ahead = first_ref[...], ahead_ref[...]
+        back, last = back_ref[...], last_ref[...]
+        turned, mixed, columns = {}, {}, {}
+
+        def enter(p):
+            held = []
+            for c in (2 * p, 2 * p + 1):
+                rows = [x_wide[j, pl.ds(base + c, blocks, stride=owned), :] for j in range(runs)]
+                held.append(jnp.concatenate(rows, axis=0).astype(BF16))
+            turned[p] = enter_pair(jnp.concatenate(held, axis=1), first, cos, sin)
+
+        def multiply(p):
+            piece, inside = divmod(base + 2 * p, PIECE)
+            if inside == 0:
+                fetched(piece).wait()
+                if (piece + 1) * PIECE < owned:
+                    fetched(piece + 1).start()
+            mixed[p] = []
+            for i in range(2):
+                rows = dot(turned[p][i], ahead)
                 re, im = rows[:, :side], rows[:, side:]
-                turned = jnp.concatenate([re * cos + im * sin, im * cos - re * sin], axis=0)
-                head, rest = split(turned)
-                columns.append(jnp.concatenate([head, rest, head], axis=0))
-            result = dot(last_ref[...], jnp.concatenate(columns, axis=1))
+                both = filt_ref[base + 2 * p + i]
+                fre, fim = both[:, :side], both[:, side:]
+                head, rest = split(
+                    jnp.concatenate([re * fre - im * fim, re * fim + im * fre], axis=1)
+                )
+                mixed[p].append(jnp.concatenate([head, rest, head], axis=1))
+
+        def undo(p):
+            both = []
+            for i in range(2):
+                rows = dot(mixed[p][i], back)
+                re, im = rows[:, :side], rows[:, side:]
+                head, rest = split(
+                    jnp.concatenate([re * cos + im * sin, im * cos - re * sin], axis=0)
+                )
+                both.append(jnp.concatenate([head, rest, head], axis=0))
+            columns[p] = jnp.concatenate(both, axis=1)
+
+        def leave(p):
+            result = dot(last, columns[p])
             for i in range(2):
                 for j in range(runs):
-                    y_wide[j, pl.ds(base + c + i, blocks, stride=owned), :] = result[
+                    y_wide[j, pl.ds(base + 2 * p + i, blocks, stride=owned), :] = result[
                         j * blocks : (j + 1) * blocks, i * side : (i + 1) * side
                     ]
+
+        stages = (enter, multiply, undo, leave)
+        pairs = GROUP // 2
+        for t in range(pairs + len(stages) - 1):
+            for late in (0, 2, 1, 3):
+                if 0 <= t - late < pairs:
+                    stages[late](t - late)
 
     part = owned // sems.shape[0]
     copies = []
     for h in range(sems.shape[0]):
-
-        @pl.loop(0, part // GROUP)
-        def _(step, h=h):
-            fetched(h * (part // GROUP) + step).wait()
+        for step in range(part // GROUP):
             some(h * part + step * GROUP)
 
-        for j in range(runs):
-            whole = y_wide[j].reshape(blocks, owned, side)
-            done[h, :, :, j * side : (j + 1) * side] = (
-                whole[:, h * part : (h + 1) * part].astype(BF16)
+        size = blocks // sems.shape[1]
+        for p in range(sems.shape[1]):
+            cut = pl.ds(p * size, size)
+            for j in range(runs):
+                rows = y_wide[j, p * size * owned : (p + 1) * size * owned]
+                rows = rows.reshape(size, owned, side)[:, h * part : (h + 1) * part]
+                done[h, cut, :, j * side : (j + 1) * side] = rows.astype(BF16)
+            copies.append(
+                pltpu.make_async_copy(
+                    done.at[h, cut], out_ref.at[cut, pl.ds(h * part, part)], sems.at[h, p]
+                )
             )
-        copies.append(
-            pltpu.make_async_copy(done.at[h], out_ref.at[:, pl.ds(h * part, part)], sems.at[h])
-        )
-        copies[-1].start()
+            copies[-1].start()
     for copy in copies:
         copy.wait()
 
@@ -337,7 +373,7 @@
             out_specs=far,
             out_shape=jax.ShapeDtypeStruct((ctx_count, held_rows, side), BF16),
             scratch_shapes=[
-                pltpu.VMEM((2, RIM + tokens, 128), F32),
+                pltpu.VMEM((4, 2, RIM + tokens, 128), F32),
                 pltpu.VMEM((2, width, tokens), BF16),
                 pltpu.VMEM((ctx_count, held_rows, side), BF16),
                 pltpu.VMEM(short_taps.shape, F32),
@@ -372,7 +408,7 @@
             out_shape=jax.ShapeDtypeStruct((owned, side, 2 * side), F32),
             scratch_shapes=[
                 pltpu.VMEM((owned, side, 2 * side), F32),
-                pltpu.SemaphoreType.DMA((owned // GROUP,)),
+                pltpu.SemaphoreType.DMA((owned // PIECE,)),
             ],
             compiler_params=params(VMEM_FILTER),
             cost_estimate=cost(owned * side**3 * 16, 5 << 20),
@@ -393,17 +429,19 @@
     with jax.named_scope("long"):
         long = pl.pallas_call(
             long_kernel,
-            in_specs=[whole, far] + [whole] * 6,
+            in_specs=[whole, far, far] + [whole] * 5,
             out_specs=far,
             out_shape=jax.ShapeDtypeStruct((ctx_count, owned, tokens), BF16),
             scratch_shapes=[
                 wide,
                 wide,
                 pltpu.VMEM((owned, side, 2 * side), F32),
+                pltpu.VMEM((2 * RIM, side), F32),
                 pltpu.VMEM((2, ctx_count * owned // side, 2 * RIM, side), F32),
                 pltpu.VMEM((parts, ctx_count, owned // parts, tokens), BF16),
-                pltpu.SemaphoreType.DMA((parts,)),
-                pltpu.SemaphoreType.DMA((owned // GROUP,)),
+                pltpu.SemaphoreType.DMA((parts, 4)),
+                pltpu.SemaphoreType.DMA((owned // PIECE,)),
+                pltpu.SemaphoreType.DMA,
             ],
             compiler_params=params(VMEM_SOME),
             cost_estimate=cost(owned * side**3 * 32, 7 << 20),

time: 72.8 us -> 70.5 us (0.968)
  Pallas kernels: 31.2 us -> 28.7 us
    pallas_call x1, Pallas kernels: 13.6 us -> 11.3 us  [local(): pl.pallas_call(long_kernel, in_specs=[whole, far, far] + [whole] * 5, out...]
  transfers between devices with their start and end apart: 3 -> 3, of which waited for: 3 -> 2; matrix products, arithmetic and copies ran while one was open for 2% -> 2% of each run, Pallas kernels for 14% -> 15%
where the time goes in v2:
time: 70.5 us; the launch traced here: 70.1 us
  Pallas kernels  28.7 us (41%)
  waiting for transfers between devices  20 us (28%)
  starting transfers between devices  19.7 us (28%)
  local copies, waits for them, and re-layouts  1.43 us (2%)
    all_to_all x1, waiting for transfers between devices, local(): lax.all_to_all(long, 'ctx', split_axis=0, concat_axis=0, tiled=True)  15 us
    pallas_call x1, Pallas kernels, local(): pl.pallas_call(long_kernel, in_specs=[whole, far, far] + [whole] * 5, out...  11.3 us
    all_to_all x1, starting transfers between devices, local(): lax.all_to_all(gated, 'ctx', split_axis=0, concat_axis=0, tiled=True)  10.7 us
    pallas_call x1, Pallas kernels, local(): pl.pallas_call(filter_kernel, in_specs=[whole, pl.BlockSpec(memory_space=...  7.81 us
    pallas_call x1, Pallas kernels, local(): pl.pallas_call(gate_kernel, in_specs=[far, far, far], out_specs=far, out_...  6.18 us
    all_to_all x1, starting transfers between devices, local(): lax.all_to_all(long, 'ctx', split_axis=0, concat_axis=0, tiled=True)  5.29 us
    all_to_all x1, waiting for transfers between devices, local(): lax.all_to_all(gated, 'ctx', split_axis=0, concat_axis=0, tiled=True)  4.96 us
    ppermute x1, starting transfers between devices, local(): query_halo = lax.ppermute(query_tail, 'ctx', shift)  3.72 us
  transfers between devices with their start and end apart: 3, of which 2 were waited for; matrix products, arithmetic and copies ran while one was open for 2% of the time, Pallas kernels for 15%

profile of v2, /device:TPU:1, one launch (start us, length us, event | category | flops | bytes accessed | tf_op | source)
XLA Modules:
  0.0 70.1 jit_solution(14904133943992700847)
XLA Ops:
  0.0 6.2 %gate.1 = bf16[64,72,128]{2,1,0:T(8,128)(2,1)} custom-call(bf16[2048,256]{1,0:T(8,128)(2,1)} %k_ref.1, bf16[2048,256]{1,0:T(8,128)(2,1)} %v_ref.1, f32[3,7,2048]{2,1,0:T(8,128)} %taps_ref.1), custom_call_target="tpu_custom_call" | custom-call | flops 15728640 | bytes 3145728 | tf_op jit(solution)/shard_map/gate/pallas_call | solution.py:370
  6.2 0.0 copy-start
  6.2 0.0 copy-start.1
  6.2 10.7 %all-to-all-start = ((bf16[64,72,128]{2,1,0:T(8,128)(2,1)}), bf16[64,72,128]{2,1,0:T(8,128)(2,1)}, u32[]{:S(2)}, u32[]{:S(2)}) async-start(bf16[64,72,128]{2,1,0:T(8,128)(2,1)} %gate.1), calls=%async_computation | async-start | bytes 2359296 | tf_op jit(solution)/shard_map/all_to_all | solution.py:387
  16.9 0.0 copy-done
  16.9 0.0 copy-start.7
  16.9 0.5 query_tail.1
  17.4 3.7 %collective-permute-start = (bf16[16,2048]{1,0:T(8,128)(2,1)S(1)}, bf16[16,2048]{1,0:T(8,128)(2,1)S(1)}, u32[]{:S(2)}, u32[]{:S(2)}) collective-permute-start(bf16[16,2048]{1,0:T(8,128)(2,1)S(1)} %query_tail.1), channel_id=1, source_target_pairs={{0,4},{4,8},{8,12},{12,16},{16,20},{20,24},{24,28},{28,32},{32,36}... | collective-permute-start | bytes 196616 | tf_op jit(solution)/shard_map/ppermute | solution.py:402
  21.1 0.0 copy-done.1
  21.1 0.1 constant_dynamic-slice_fusion
  21.2 0.1 tile.12.far_taps_ref
  21.3 0.0 copy-done.7
  21.3 1.2 %copy.13 = bf16[4,8,128,128]{3,2,1,0:T(8,128)(2,1)} copy(bf16[4,8,128,128]{3,1,2,0:T(8,128)(2,1)S(1)} %bitcast.8) | data formatting | bytes 2097152
  22.5 0.0 copy-start.2
  22.5 0.0 copy-start.3
  22.5 0.0 copy-start.4
  22.5 0.0 copy-start.5
  22.5 0.0 copy-start.6
  22.5 7.8 %filter.1.far_ref = f32[32,128,256]{2,1,0:T(8,128)} custom-call(bf16[32,128,128]{2,1,0:T(8,128)(2,1)} %bitcast.7, f32[1,32]{1,0:T(1,128)} %gain_ref.1, bf16[256,256]{1,0:T(8,128)(2,1)} %constant.26.clone.first_ref, f32[2,128,128]{2,1,0:T(8,128)} %constant.28.clone.twist_ref, bf16[768,256]{1,0:T(8,128)(2,1)} %constant.29.clone.ahead_ref), custom_call_target="tpu_custom_call" | custom-call | flops 1073741824 | bytes 5242880 | tf_op jit(solution)/shard_map/filter/pallas_call | solution.py:404
  30.4 0.0 collective-permute-done.halo_ref
  30.4 5.0 %all-to-all-done.x_ref = bf16[64,72,128]{2,1,0:T(8,128)(2,1)} async-done(((bf16[64,72,128]{2,1,0:T(8,128)(2,1)}), bf16[64,72,128]{2,1,0:T(8,128)(2,1)}, u32[]{:S(2)}, u32[]{:S(2)}) %all-to-all-start) | async-done | bytes 1179680 | tf_op jit(solution)/shard_map/all_to_all | solution.py:387
  35.3 0.0 copy-done.2
  35.3 0.0 copy-done.3
  35.3 0.0 copy-done.4
  35.3 0.0 copy-done.5
  35.4 0.0 copy-done.6
  35.4 11.3 %long.1 = bf16[64,32,256]{2,1,0:T(8,128)(2,1)} custom-call(bf16[64,72,128]{2,1,0:T(8,128)(2,1)} %all-to-all-done.x_ref, f32[32,128,256]{2,1,0:T(8,128)} %filter.1.far_ref, f32[16,128]{1,0:T(8,128)S(1)} %tile.12.far_taps_ref, bf16[256,256]{1,0:T(8,128)(2,1)S(1)} %copy-done.6, f32[2,128,128]{2,1,0:T(8,128)S(1)} %copy-done.3, bf16[768,256]{1,0:T(8,128)(2,1)S(1)} %copy-done.2, ...), custom_call_target="tpu_custom_call" | custom-call | flops 2147483648 | bytes 7340032 | tf_op jit(solution)/shard_map/long/pallas_call | solution.py:430
  46.6 5.3 %all-to-all-start.1 = ((bf16[64,32,256]{2,1,0:T(8,128)(2,1)}), bf16[64,32,256]{2,1,0:T(8,128)(2,1)S(1)}, u32[]{:S(2)}, u32[]{:S(2)}) async-start(bf16[64,32,256]{2,1,0:T(8,128)(2,1)} %long.1), calls=%async_computation.1 | async-start | bytes 2097152 | tf_op jit(solution)/shard_map/all_to_all | solution.py:449
  51.9 1.9 %query.1.q_ref = bf16[2048,256]{1,0:T(8,128)(2,1)S(1)} custom-call(bf16[2048,256]{1,0:T(8,128)(2,1)S(1)} %copy-done, bf16[16,2048]{1,0:T(8,128)(2,1)S(1)} %collective-permute-done.halo_ref, f32[3,7,2048]{2,1,0:T(8,128)S(1)} %copy-done.1), custom_call_target="tpu_custom_call" | custom-call | flops 7864320 | bytes 2097152 | tf_op jit(solution)/shard_map/query/pallas_call | solution.py:418
  53.9 15.0 %all-to-all-done.1 = bf16[64,32,256]{2,1,0:T(8,128)(2,1)S(1)} async-done(((bf16[64,32,256]{2,1,0:T(8,128)(2,1)}), bf16[64,32,256]{2,1,0:T(8,128)(2,1)S(1)}, u32[]{:S(2)}, u32[]{:S(2)}) %all-to-all-start.1) | async-done | bytes 1048608 | tf_op jit(solution)/shard_map/all_to_all | solution.py:449
  68.9 1.1 %product.1 = bf16[2048,256]{1,0:T(8,128)(2,1)} custom-call(bf16[2048,256]{1,0:T(8,128)(2,1)S(1)} %query.1.q_ref, bf16[2048,256]{1,0:T(8,128)(2,1)S(1)} %bitcast.6), custom_call_target="tpu_custom_call" | custom-call | flops 524288 | bytes 3145728 | tf_op jit(solution)/shard_map/product/pallas_call | solution.py:452
  (2 shorter events, 0.0 us)
Async XLA Ops:
  6.2 10.7 %copy-start = (bf16[2048,256]{1,0:T(8,128)(2,1)S(1)}, bf16[2048,256]{1,0:T(8,128)(2,1)}, u32[]{:S(2)}) copy-start(bf16[2048,256]{1,0:T(8,128)(2,1)} %q_ref.1) | copy-start | bytes 3145732
  6.2 14.9 %copy-start.1 = (f32[3,7,2048]{2,1,0:T(8,128)S(1)}, f32[3,7,2048]{2,1,0:T(8,128)}, u32[]{:S(2)}) copy-start(f32[3,7,2048]{2,1,0:T(8,128)} %taps_ref.1) | copy-start | bytes 516100
  6.2 29.1 %all-to-all-start = ((bf16[64,72,128]{2,1,0:T(8,128)(2,1)}), bf16[64,72,128]{2,1,0:T(8,128)(2,1)}, u32[]{:S(2)}, u32[]{:S(2)}) async-start(bf16[64,72,128]{2,1,0:T(8,128)(2,1)} %gate.1), calls=%async_computation | async-start | bytes 2359296 | tf_op jit(solution)/shard_map/all_to_all | solution.py:387
  16.9 4.4 %copy-start.7 = (bf16[1,32,16384]{2,1,0:T(8,128)(2,1)S(1)}, bf16[1,32,16384]{2,1,0:T(8,128)(2,1)}, u32[]{:S(2)}) copy-start(bf16[1,32,16384]{2,1,0:T(8,128)(2,1)} %param.16) | copy-start | bytes 3145732
  17.4 13.0 %collective-permute-start = (bf16[16,2048]{1,0:T(8,128)(2,1)S(1)}, bf16[16,2048]{1,0:T(8,128)(2,1)S(1)}, u32[]{:S(2)}, u32[]{:S(2)}) collective-permute-start(bf16[16,2048]{1,0:T(8,128)(2,1)S(1)} %query_tail.1), channel_id=1, source_target_pairs={{0,4},{4,8},{8,12},{12,16},{16,20},{20,24},{24,28},{28,32},{32,36}... | collective-permute-start | bytes 196616 | tf_op jit(solution)/shard_map/ppermute | solution.py:402
  22.5 12.8 %copy-start.2 = (bf16[768,256]{1,0:T(8,128)(2,1)S(1)}, bf16[768,256]{1,0:T(8,128)(2,1)}, u32[]{:S(2)}) copy-start(bf16[768,256]{1,0:T(8,128)(2,1)} %constant.29.clone.ahead_ref) | copy-start | bytes 1179652
  22.5 12.8 %copy-start.3 = (f32[2,128,128]{2,1,0:T(8,128)S(1)}, f32[2,128,128]{2,1,0:T(8,128)}, u32[]{:S(2)}) copy-start(f32[2,128,128]{2,1,0:T(8,128)} %constant.28.clone.twist_ref) | copy-start | bytes 393220
  22.5 12.8 %copy-start.4 = (bf16[768,256]{1,0:T(8,128)(2,1)S(1)}, bf16[768,256]{1,0:T(8,128)(2,1)}, u32[]{:S(2)}) copy-start(bf16[768,256]{1,0:T(8,128)(2,1)} %constant.30.clone.back_ref) | copy-start | bytes 1179652
  22.5 12.8 %copy-start.5 = (bf16[128,768]{1,0:T(8,128)(2,1)S(1)}, bf16[128,768]{1,0:T(8,128)(2,1)}, u32[]{:S(2)}) copy-start(bf16[128,768]{1,0:T(8,128)(2,1)} %constant.31.clone.last_ref) | copy-start | bytes 589828
  22.5 12.8 %copy-start.6 = (bf16[256,256]{1,0:T(8,128)(2,1)S(1)}, bf16[256,256]{1,0:T(8,128)(2,1)}, u32[]{:S(2)}) copy-start(bf16[256,256]{1,0:T(8,128)(2,1)} %constant.27.clone.first_ref) | copy-start | bytes 393220
  46.6 22.2 %all-to-all-start.1 = ((bf16[64,32,256]{2,1,0:T(8,128)(2,1)}), bf16[64,32,256]{2,1,0:T(8,128)(2,1)S(1)}, u32[]{:S(2)}, u32[]{:S(2)}) async-start(bf16[64,32,256]{2,1,0:T(8,128)(2,1)} %long.1), calls=%async_computation.1 | async-start | bytes 2097152 | tf_op jit(solution)/shard_map/all_to_all | solution.py:449

commit v3 on v2

--- a/solution.py
+++ b/solution.py
@@ -13,7 +13,7 @@
 RIM = 8
 TAPS = 7
 GROUP = 16
-PIECE = 8
+PIECE = 4
 BF16, F32 = jnp.bfloat16, jnp.float32
 
 

time: 70.5 us -> 71.7 us (1.017)
  Pallas kernels: 28.7 us -> 30.1 us
    pallas_call x1, Pallas kernels: 11.3 us -> 12.2 us  [local(): pl.pallas_call(long_kernel, in_specs=[whole, far, far] + [whole] * 5, out...]
where the time goes in v3:
time: 71.7 us; the launch traced here: 71.1 us
  Pallas kernels  30.1 us (42%)
  starting transfers between devices  19.7 us (27%)
  waiting for transfers between devices  19.5 us (27%)
  local copies, waits for them, and re-layouts  1.43 us (2%)
    all_to_all x1, waiting for transfers between devices, local(): lax.all_to_all(long, 'ctx', split_axis=0, concat_axis=0, tiled=True)  15 us
    pallas_call x1, Pallas kernels, local(): pl.pallas_call(long_kernel, in_specs=[whole, far, far] + [whole] * 5, out...  12.2 us
    all_to_all x1, starting transfers between devices, local(): lax.all_to_all(gated, 'ctx', split_axis=0, concat_axis=0, tiled=True)  10.7 us
    pallas_call x1, Pallas kernels, local(): pl.pallas_call(filter_kernel, in_specs=[whole, pl.BlockSpec(memory_space=...  8.24 us
    pallas_call x1, Pallas kernels, local(): pl.pallas_call(gate_kernel, in_specs=[far, far, far], out_specs=far, out_...  6.18 us
    all_to_all x1, starting transfers between devices, local(): lax.all_to_all(long, 'ctx', split_axis=0, concat_axis=0, tiled=True)  5.29 us
    all_to_all x1, waiting for transfers between devices, local(): lax.all_to_all(gated, 'ctx', split_axis=0, concat_axis=0, tiled=True)  4.53 us
    ppermute x1, starting transfers between devices, local(): query_halo = lax.ppermute(query_tail, 'ctx', shift)  3.72 us
  transfers between devices with their start and end apart: 3, of which 2 were waited for; matrix products, arithmetic and copies ran while one was open for 2% of the time, Pallas kernels for 15%

profile of v3, /device:TPU:1, one launch (start us, length us, event | category | flops | bytes accessed | tf_op | source)
XLA Modules:
  0.0 71.1 jit_solution(13508366782544309810)
XLA Ops:
  0.0 6.2 %gate.1 = bf16[64,72,128]{2,1,0:T(8,128)(2,1)} custom-call(bf16[2048,256]{1,0:T(8,128)(2,1)} %k_ref.1, bf16[2048,256]{1,0:T(8,128)(2,1)} %v_ref.1, f32[3,7,2048]{2,1,0:T(8,128)} %taps_ref.1), custom_call_target="tpu_custom_call" | custom-call | flops 15728640 | bytes 3145728 | tf_op jit(solution)/shard_map/gate/pallas_call | solution.py:370
  6.2 0.0 copy-start
  6.2 0.0 copy-start.1
  6.2 10.7 %all-to-all-start = ((bf16[64,72,128]{2,1,0:T(8,128)(2,1)}), bf16[64,72,128]{2,1,0:T(8,128)(2,1)}, u32[]{:S(2)}, u32[]{:S(2)}) async-start(bf16[64,72,128]{2,1,0:T(8,128)(2,1)} %gate.1), calls=%async_computation | async-start | bytes 2359296 | tf_op jit(solution)/shard_map/all_to_all | solution.py:387
  16.9 0.0 copy-done
  16.9 0.0 copy-start.7
  16.9 0.5 query_tail.1
  17.4 3.7 %collective-permute-start = (bf16[16,2048]{1,0:T(8,128)(2,1)S(1)}, bf16[16,2048]{1,0:T(8,128)(2,1)S(1)}, u32[]{:S(2)}, u32[]{:S(2)}) collective-permute-start(bf16[16,2048]{1,0:T(8,128)(2,1)S(1)} %query_tail.1), channel_id=1, source_target_pairs={{0,4},{4,8},{8,12},{12,16},{16,20},{20,24},{24,28},{28,32},{32,36}... | collective-permute-start | bytes 196616 | tf_op jit(solution)/shard_map/ppermute | solution.py:402
  21.1 0.0 copy-done.1
  21.1 0.1 constant_dynamic-slice_fusion
  21.2 0.1 tile.12.far_taps_ref
  21.3 0.0 copy-done.7
  21.3 1.2 %copy.13 = bf16[4,8,128,128]{3,2,1,0:T(8,128)(2,1)} copy(bf16[4,8,128,128]{3,1,2,0:T(8,128)(2,1)S(1)} %bitcast.8) | data formatting | bytes 2097152
  22.5 0.0 copy-start.2
  22.5 0.0 copy-start.3
  22.5 0.0 copy-start.4
  22.5 0.0 copy-start.5
  22.5 0.0 copy-start.6
  22.5 8.2 %filter.1.far_ref = f32[32,128,256]{2,1,0:T(8,128)} custom-call(bf16[32,128,128]{2,1,0:T(8,128)(2,1)} %bitcast.7, f32[1,32]{1,0:T(1,128)} %gain_ref.1, bf16[256,256]{1,0:T(8,128)(2,1)} %constant.26.clone.first_ref, f32[2,128,128]{2,1,0:T(8,128)} %constant.28.clone.twist_ref, bf16[768,256]{1,0:T(8,128)(2,1)} %constant.29.clone.ahead_ref), custom_call_target="tpu_custom_call" | custom-call | flops 1073741824 | bytes 5242880 | tf_op jit(solution)/shard_map/filter/pallas_call | solution.py:404
  30.8 0.0 collective-permute-done.halo_ref
  30.8 4.5 %all-to-all-done.x_ref = bf16[64,72,128]{2,1,0:T(8,128)(2,1)} async-done(((bf16[64,72,128]{2,1,0:T(8,128)(2,1)}), bf16[64,72,128]{2,1,0:T(8,128)(2,1)}, u32[]{:S(2)}, u32[]{:S(2)}) %all-to-all-start) | async-done | bytes 1179680 | tf_op jit(solution)/shard_map/all_to_all | solution.py:387
  35.3 0.0 copy-done.2
  35.3 0.0 copy-done.3
  35.3 0.0 copy-done.4
  35.3 0.0 copy-done.5
  35.4 0.0 copy-done.6
  35.4 12.2 %long.1 = bf16[64,32,256]{2,1,0:T(8,128)(2,1)} custom-call(bf16[64,72,128]{2,1,0:T(8,128)(2,1)} %all-to-all-done.x_ref, f32[32,128,256]{2,1,0:T(8,128)} %filter.1.far_ref, f32[16,128]{1,0:T(8,128)S(1)} %tile.12.far_taps_ref, bf16[256,256]{1,0:T(8,128)(2,1)S(1)} %copy-done.6, f32[2,128,128]{2,1,0:T(8,128)S(1)} %copy-done.3, bf16[768,256]{1,0:T(8,128)(2,1)S(1)} %copy-done.2, ...), custom_call_target="tpu_custom_call" | custom-call | flops 2147483648 | bytes 7340032 | tf_op jit(solution)/shard_map/long/pallas_call | solution.py:430
  47.6 5.3 %all-to-all-start.1 = ((bf16[64,32,256]{2,1,0:T(8,128)(2,1)}), bf16[64,32,256]{2,1,0:T(8,128)(2,1)S(1)}, u32[]{:S(2)}, u32[]{:S(2)}) async-start(bf16[64,32,256]{2,1,0:T(8,128)(2,1)} %long.1), calls=%async_computation.1 | async-start | bytes 2097152 | tf_op jit(solution)/shard_map/all_to_all | solution.py:449
  52.9 1.9 %query.1.q_ref = bf16[2048,256]{1,0:T(8,128)(2,1)S(1)} custom-call(bf16[2048,256]{1,0:T(8,128)(2,1)S(1)} %copy-done, bf16[16,2048]{1,0:T(8,128)(2,1)S(1)} %collective-permute-done.halo_ref, f32[3,7,2048]{2,1,0:T(8,128)S(1)} %copy-done.1), custom_call_target="tpu_custom_call" | custom-call | flops 7864320 | bytes 2097152 | tf_op jit(solution)/shard_map/query/pallas_call | solution.py:418
  54.8 15.0 %all-to-all-done.1 = bf16[64,32,256]{2,1,0:T(8,128)(2,1)S(1)} async-done(((bf16[64,32,256]{2,1,0:T(8,128)(2,1)}), bf16[64,32,256]{2,1,0:T(8,128)(2,1)S(1)}, u32[]{:S(2)}, u32[]{:S(2)}) %all-to-all-start.1) | async-done | bytes 1048608 | tf_op jit(solution)/shard_map/all_to_all | solution.py:449
  69.8 1.1 %product.1 = bf16[2048,256]{1,0:T(8,128)(2,1)} custom-call(bf16[2048,256]{1,0:T(8,128)(2,1)S(1)} %query.1.q_ref, bf16[2048,256]{1,0:T(8,128)(2,1)S(1)} %bitcast.6), custom_call_target="tpu_custom_call" | custom-call | flops 524288 | bytes 3145728 | tf_op jit(solution)/shard_map/product/pallas_call | solution.py:452
  (2 shorter events, 0.0 us)
Async XLA Ops:
  6.2 10.7 %copy-start = (bf16[2048,256]{1,0:T(8,128)(2,1)S(1)}, bf16[2048,256]{1,0:T(8,128)(2,1)}, u32[]{:S(2)}) copy-start(bf16[2048,256]{1,0:T(8,128)(2,1)} %q_ref.1) | copy-start | bytes 3145732
  6.2 14.9 %copy-start.1 = (f32[3,7,2048]{2,1,0:T(8,128)S(1)}, f32[3,7,2048]{2,1,0:T(8,128)}, u32[]{:S(2)}) copy-start(f32[3,7,2048]{2,1,0:T(8,128)} %taps_ref.1) | copy-start | bytes 516100
  6.2 29.1 %all-to-all-start = ((bf16[64,72,128]{2,1,0:T(8,128)(2,1)}), bf16[64,72,128]{2,1,0:T(8,128)(2,1)}, u32[]{:S(2)}, u32[]{:S(2)}) async-start(bf16[64,72,128]{2,1,0:T(8,128)(2,1)} %gate.1), calls=%async_computation | async-start | bytes 2359296 | tf_op jit(solution)/shard_map/all_to_all | solution.py:387
  16.9 4.4 %copy-start.7 = (bf16[1,32,16384]{2,1,0:T(8,128)(2,1)S(1)}, bf16[1,32,16384]{2,1,0:T(8,128)(2,1)}, u32[]{:S(2)}) copy-start(bf16[1,32,16384]{2,1,0:T(8,128)(2,1)} %param.16) | copy-start | bytes 3145732
  17.4 13.4 %collective-permute-start = (bf16[16,2048]{1,0:T(8,128)(2,1)S(1)}, bf16[16,2048]{1,0:T(8,128)(2,1)S(1)}, u32[]{:S(2)}, u32[]{:S(2)}) collective-permute-start(bf16[16,2048]{1,0:T(8,128)(2,1)S(1)} %query_tail.1), channel_id=1, source_target_pairs={{0,4},{4,8},{8,12},{12,16},{16,20},{20,24},{24,28},{28,32},{32,36}... | collective-permute-start | bytes 196616 | tf_op jit(solution)/shard_map/ppermute | solution.py:402
  22.5 12.8 %copy-start.2 = (bf16[768,256]{1,0:T(8,128)(2,1)S(1)}, bf16[768,256]{1,0:T(8,128)(2,1)}, u32[]{:S(2)}) copy-start(bf16[768,256]{1,0:T(8,128)(2,1)} %constant.29.clone.ahead_ref) | copy-start | bytes 1179652
  22.5 12.8 %copy-start.3 = (f32[2,128,128]{2,1,0:T(8,128)S(1)}, f32[2,128,128]{2,1,0:T(8,128)}, u32[]{:S(2)}) copy-start(f32[2,128,128]{2,1,0:T(8,128)} %constant.28.clone.twist_ref) | copy-start | bytes 393220
  22.5 12.8 %copy-start.4 = (bf16[768,256]{1,0:T(8,128)(2,1)S(1)}, bf16[768,256]{1,0:T(8,128)(2,1)}, u32[]{:S(2)}) copy-start(bf16[768,256]{1,0:T(8,128)(2,1)} %constant.30.clone.back_ref) | copy-start | bytes 1179652
  22.5 12.8 %copy-start.5 = (bf16[128,768]{1,0:T(8,128)(2,1)S(1)}, bf16[128,768]{1,0:T(8,128)(2,1)}, u32[]{:S(2)}) copy-start(bf16[128,768]{1,0:T(8,128)(2,1)} %constant.31.clone.last_ref) | copy-start | bytes 589828
  22.5 12.8 %copy-start.6 = (bf16[256,256]{1,0:T(8,128)(2,1)S(1)}, bf16[256,256]{1,0:T(8,128)(2,1)}, u32[]{:S(2)}) copy-start(bf16[256,256]{1,0:T(8,128)(2,1)} %constant.27.clone.first_ref) | copy-start | bytes 393220
  47.6 22.2 %all-to-all-start.1 = ((bf16[64,32,256]{2,1,0:T(8,128)(2,1)}), bf16[64,32,256]{2,1,0:T(8,128)(2,1)S(1)}, u32[]{:S(2)}, u32[]{:S(2)}) async-start(bf16[64,32,256]{2,1,0:T(8,128)(2,1)} %long.1), calls=%async_computation.1 | async-start | bytes 2097152 | tf_op jit(solution)/shard_map/all_to_all | solution.py:449
